TPU v7x, 512 devices: a whole 4x4x16 slice. The times are simulated.
512 devices in a mesh: enc: 2 (over core), blk: 8 (over y_lo, x), voc: 32 (over z, y_hi).
Axes of the slice: x: 4, y: 4 (y_hi: 2, y_lo: 2; y = y_hi * 2 + y_lo), z: 16, core: 2. Of those that a mesh axis runs over, the one named last changes fastest.
Arguments:
- queries: bfloat16 [16384, 2048], P(('blk', 'voc'), 'enc'), may hold values from -100 to 100
- residual: bfloat16 [16384, 2048], P(('blk', 'voc'), 'enc'), may hold values from -6 to 6
- mem_keys: bfloat16 [8192, 2048], P(('blk', 'voc'), 'enc'), may hold values from -6 to 6
- mem_values: bfloat16 [8192, 2048], P(('blk', 'voc'), 'enc'), may hold values from -6 to 6
- dec_ids: int32 [16384], P(('blk', 'voc')), may hold values from 0 to 31, as said below
- mem_ids: int32 [8192], P(('blk', 'voc')), may hold values from 0 to 31, as said below
- targets: int32 [16384], P(('blk', 'voc')), may hold values from 0 to 32767
- ln_gain: float32 [2048], replicated, may hold values from 0.5 to 1.5
- ln_bias: float32 [2048], replicated, may hold values from -3 to 3
- head_weight: bfloat16 [2048, 32768], P(None, ('enc', 'voc')), may hold values from -1 to 1
Outputs:
- row_loss: float32 [16384], P(('blk', 'voc'))
Inputs may be any that keep to these rules, and one draw needn't show every extreme that they name: `dec_ids`: within each block of 2048 decoder rows the numbers never fall, start at 0 and end at 31, and each of the 32 sentences has at least one row. `mem_ids`: within each block of 1024 memory rows the numbers never fall, start at 0 and end at 31, and each of the 32 sentences has at least one row.
All inputs are finite; a program needn't handle non-finite values.
Results may differ from a plain program's by a relative error of at most 0.003.
Values may be sent and summed in bfloat16 or wider, within the bound.
No kernel may reach another device: no remote copies, remote signals or barrier semaphores. Data moves between devices by JAX's collectives and lax.ppermute only.
A program may use at most 64 MiB of HBM per device.

v0:
```python
import math

import jax
import jax.numpy as jnp
from jax import lax
from jax.sharding import PartitionSpec as P

D = 2048
HEADS = 16


EPS_SMOOTH = 0.1
Z_COEF = 0.0001
LN_EPS = 1e-05


def joined(part, axis, combine):
    gathered = jax.tree.map(lambda a: lax.all_gather(a, axis), part)

    def take(source):
        return jax.tree.map(lambda a: lax.dynamic_index_in_dim(a, source, 0, False), gathered)

    return lax.fori_loop(
        1, lax.axis_size(axis), lambda source, state: combine(state, take(source)), take(0)
    )


def row_stats(block_rows, block_targets, head_weight, slab_start):
    logits = jnp.dot(block_rows, head_weight, preferred_element_type=jnp.float32)
    top_logit = jnp.max(logits, axis=1)
    exp_total = jnp.sum(jnp.exp(logits - top_logit[:, None]), axis=1)
    logit_sum = jnp.sum(logits, axis=1)
    positions = slab_start + lax.broadcasted_iota(jnp.int32, logits.shape, 1)
    picked = jnp.sum(jnp.where(positions == block_targets[:, None], logits, 0.0), axis=1)
    return (top_logit, exp_total, logit_sum, picked)


def combine_stats(earlier, later):
    top_logit = jnp.maximum(earlier[0], later[0])
    exp_total = earlier[1] * jnp.exp(earlier[0] - top_logit) + later[1] * jnp.exp(
        later[0] - top_logit
    )
    return (top_logit, exp_total, earlier[2] + later[2], earlier[3] + later[3])


def per_device(
    queries,
    residual,
    mem_keys,
    mem_values,
    dec_ids,
    mem_ids,
    targets,
    ln_gain,
    ln_bias,
    head_weight,
):
    row_count, half_width = queries.shape
    head_dim = D // HEADS
    heads_here = half_width // head_dim
    keys_all, values_all, ids_all = (
        lax.all_gather(mem_keys, "voc", axis=0, tiled=True),
        lax.all_gather(mem_values, "voc", axis=0, tiled=True),
        lax.all_gather(mem_ids, "voc", axis=0, tiled=True),
    )
    query_heads = queries.reshape(row_count, heads_here, head_dim)
    key_heads = keys_all.reshape(-1, heads_here, head_dim)
    value_heads = values_all.reshape(-1, heads_here, head_dim)
    scores = jnp.einsum("ihd,jhd->hij", query_heads, key_heads, preferred_element_type=jnp.float32)
    scores = scores * (1.0 / math.sqrt(head_dim))
    allowed = dec_ids[:, None] == ids_all[None, :]
    scores = jnp.where(allowed[None], scores, -jnp.inf)
    top_score = jnp.max(scores, axis=2, keepdims=True)
    raised = jnp.exp(scores - top_score)
    weights = (raised / jnp.sum(raised, axis=2, keepdims=True)).astype(jnp.bfloat16)
    context = jnp.einsum("hij,jhd->ihd", weights, value_heads, preferred_element_type=jnp.float32)
    context = context.reshape(row_count, half_width).astype(jnp.bfloat16)
    summed = (residual.astype(jnp.float32) + context.astype(jnp.float32)).astype(jnp.bfloat16)
    full_rows = lax.all_gather(summed, "enc", axis=1, tiled=True).astype(jnp.float32)
    row_mean = jnp.mean(full_rows, axis=1, keepdims=True)
    centered = full_rows - row_mean
    row_var = jnp.mean(centered * centered, axis=1, keepdims=True)
    normed = (centered * lax.rsqrt(row_var + LN_EPS) * ln_gain + ln_bias).astype(jnp.bfloat16)
    enc_count = lax.axis_size("enc")
    voc_count = lax.axis_size("voc")
    slab_width = head_weight.shape[1]
    slab_start = (lax.axis_index("enc") * voc_count + lax.axis_index("voc")) * slab_width
    found = row_stats(
        lax.all_gather(normed, "voc", axis=0, tiled=True),
        lax.all_gather(targets, "voc", axis=0, tiled=True),
        head_weight,
        slab_start,
    )
    stats = tuple((fresh for fresh in found))
    merged = joined(stats, ("enc", "voc"), combine_stats)
    own_rows = lax.axis_index("voc") * row_count
    top_logit, exp_total, logit_sum, picked = tuple(
        (lax.dynamic_slice_in_dim(item, own_rows, row_count, 0) for item in merged)
    )
    vocab_total = slab_width * enc_count * voc_count
    log_total = top_logit + jnp.log(exp_total)
    return (
        (1.0 - EPS_SMOOTH) * (log_total - picked)
        + EPS_SMOOTH * (log_total - logit_sum / vocab_total)
        + Z_COEF * log_total * log_total
    )


def solution(mesh):
    in_specs = (
        P(("blk", "voc"), "enc"),
        P(("blk", "voc"), "enc"),
        P(("blk", "voc"), "enc"),
        P(("blk", "voc"), "enc"),
        P(("blk", "voc")),
        P(("blk", "voc")),
        P(("blk", "voc")),
        P(),
        P(),
        P(None, ("enc", "voc")),
    )
    out_specs = P(("blk", "voc"))
    return jax.shard_map(
        per_device, mesh=mesh, in_specs=in_specs, out_specs=out_specs, check_vma=False
    )
```

profile of v0, /device:TPU:1, one launch (start us, length us, event | category | flops | bytes accessed | tf_op | source)
XLA Modules:
  0.0 1218.9 jit_solution(7620437530312198366)
XLA Ops:
  8.1 1.3 dynamic-slice
  12.4 127.9 %all-reduce.2 = (s32[1024]{0:T(1024)S(1)}, s32[2048]{0:T(1024)S(1)}) all-reduce(s32[1024]{0:T(1024)S(1)} %dynamic-update-slice, s32[2048]{0:T(1024)S(1)} %dynamic-update-slice.1), channel_id=1, replica_groups=mesh['enc'=2,'blk'=8,'voc'=32] {'voc'}, use_global_device_ids=true, to_apply=%add | all-reduce | flops 3072 | bytes 24576
  141.1 16.7 %all-gather.8.cloned.1.call-done = bf16[1024,1024]{1,0:T(8,128)(2,1)} async-done(((bf16[32,1024]{1,0:T(8,128)(2,1)}), bf16[1024,1024]{1,0:T(8,128)(2,1)}) %all-gather.8.cloned.1.call-update) | async-done | bytes 2097168 | tf_op jit(solution)/shard_map/all_gather | solution.py:62
  157.8 3.9 copy.18
  161.7 2.0 fusion.14
  163.8 1.3 copy-done.1
  165.8 139.3 %all-gather.10.cloned.1.call-done = bf16[1024,1024]{1,0:T(8,128)(2,1)} async-done(((bf16[32,1024]{1,0:T(8,128)(2,1)}), bf16[1024,1024]{1,0:T(8,128)(2,1)}) %all-gather.10.cloned.1.call-update) | async-done | bytes 2097168 | tf_op jit(solution)/shard_map/all_gather | solution.py:63
  305.1 4.0 copy.21
  309.0 3.3 fusion.3
  312.3 11.4 all_gather.45
  325.1 179.6 %all-gather.12.cloned.1.call-done = bf16[2048,2048]{1,0:T(8,128)(2,1)} async-done(((bf16[64,2048]{1,0:T(8,128)(2,1)}), bf16[2048,2048]{1,0:T(8,128)(2,1)}) %all-gather.12.cloned.1.call-update) | async-done | bytes 8388624 | tf_op jit(solution)/shard_map/all_gather | solution.py:89
  504.7 7.0 fusion.25
  511.7 1.4 select_reduce_fusion
  513.1 147.1 %all-gather.2 = f32[131072]{0:T(1024)S(1)} all-gather(f32[2048]{0:T(1024)S(1)} %get-tuple-element.233), channel_id=4, replica_groups=mesh['enc'=2,'blk'=8,'voc'=32] {'enc','voc'}, dimensions={0}, use_global_device_ids=true | all-gather | bytes 532480 | tf_op jit(solution)/shard_map/all_gather | solution.py:18
  660.3 144.4 %all-gather.3 = f32[131072]{0:T(1024)S(1)} all-gather(f32[2048]{0:T(1024)S(1)} %get-tuple-element.232), channel_id=5, replica_groups=mesh['enc'=2,'blk'=8,'voc'=32] {'enc','voc'}, dimensions={0}, use_global_device_ids=true | all-gather | bytes 532480 | tf_op jit(solution)/shard_map/all_gather | solution.py:18
  804.7 0.9 reshape.65
  805.6 145.0 %all-gather.1 = f32[131072]{0:T(1024)S(1)} all-gather(f32[2048]{0:T(1024)S(1)} %get-tuple-element.234), channel_id=3, replica_groups=mesh['enc'=2,'blk'=8,'voc'=32] {'enc','voc'}, dimensions={0}, use_global_device_ids=true | all-gather | bytes 532480 | tf_op jit(solution)/shard_map/all_gather | solution.py:18
  950.6 0.9 reshape.63
  951.5 144.5 %all-gather = f32[131072]{0:T(1024)S(1)} all-gather(f32[2048]{0:T(1024)S(1)} %get-tuple-element.261), channel_id=2, replica_groups=mesh['enc'=2,'blk'=8,'voc'=32] {'enc','voc'}, dimensions={0}, use_global_device_ids=true | all-gather | bytes 532480 | tf_op jit(solution)/shard_map/all_gather | solution.py:18
  1096.9 114.9 %while.21 = (s32[]{:T(128)}, f32[2048]{0:T(1024)S(1)}, f32[2048]{0:T(1024)S(1)}, f32[2048]{0:T(1024)S(1)}, f32[2048]{0:T(1024)S(1)}, /*index=5*/f32[64,2048]{1,0...) while((s32[]{:T(128)}, f32[2048]{0:T(1024)S(1)}, ...), condition=%wide.region_9.10_spmd, body=%wide.region_8.9_spmd.sunk | while | flops 16389 | bytes 164007 | solution.py:23
  1100.5 0.9 constant_dynamic-slice_fusion.6
  1104.1 0.9 constant_dynamic-slice_fusion.6
  1107.8 0.9 constant_dynamic-slice_fusion.6
  1111.4 0.9 constant_dynamic-slice_fusion.6
  1115.1 0.9 constant_dynamic-slice_fusion.6
  1118.7 0.9 constant_dynamic-slice_fusion.6
  1120.6 0.9 constant_dynamic-slice_fusion.6
  1122.4 0.9 constant_dynamic-slice_fusion.6
  1124.2 0.9 constant_dynamic-slice_fusion.6
  1127.9 0.9 constant_dynamic-slice_fusion.6
  1131.5 0.9 constant_dynamic-slice_fusion.6
  1135.2 0.9 constant_dynamic-slice_fusion.6
  1138.8 0.9 constant_dynamic-slice_fusion.6
  1142.5 0.9 constant_dynamic-slice_fusion.6
  1146.1 0.9 constant_dynamic-slice_fusion.6
  1149.7 0.9 constant_dynamic-slice_fusion.6
  1153.4 0.9 constant_dynamic-slice_fusion.6
  1155.2 0.9 constant_dynamic-slice_fusion.6
  1157.0 0.9 constant_dynamic-slice_fusion.6
  1158.9 0.9 constant_dynamic-slice_fusion.6
  1162.5 0.9 constant_dynamic-slice_fusion.6
  1166.2 0.9 constant_dynamic-slice_fusion.6
  1169.8 0.9 constant_dynamic-slice_fusion.6
  1173.5 0.9 constant_dynamic-slice_fusion.6
  1177.1 0.9 constant_dynamic-slice_fusion.6
  1180.8 0.9 constant_dynamic-slice_fusion.6
  1184.4 0.9 constant_dynamic-slice_fusion.6
  1188.1 0.9 constant_dynamic-slice_fusion.6
  (324 shorter events, 94.5 us)
Async XLA Ops:
  6.5 498.2 %copy-start = (bf16[2048,512]{1,0:T(8,128)(2,1)S(1)}, bf16[2048,512]{1,0:T(8,128)(2,1)}, u32[]{:S(2)}) copy-start(bf16[2048,512]{1,0:T(8,128)(2,1)} %param.21) | copy-start | bytes 6291460
  6.5 151.3 %all-gather.8.cloned.1.call-start = ((), (), s32[]{:S(2)}) async-start(), calls=%async_computation | async-start | bytes 2162688 | tf_op jit(solution)/shard_map/all_gather | solution.py:62
  7.3 297.8 %all-gather.10.cloned.1.call-start = ((), (), s32[]{:S(2)}) async-start(), calls=%async_computation.1 | async-start | bytes 2162688 | tf_op jit(solution)/shard_map/all_gather | solution.py:63
  8.0 496.7 %all-gather.12.cloned.1.call-start = ((), (), s32[]{:S(2)}) async-start(), calls=%async_computation.2 | async-start | bytes 8650752 | tf_op jit(solution)/shard_map/all_gather | solution.py:89
  141.1 20.7 %copy-start.2 = (bf16[64,1024]{1,0:T(8,128)(2,1)S(1)}, bf16[64,1024]{1,0:T(8,128)(2,1)}, u32[]{:S(2)}) copy-start(bf16[64,1024]{1,0:T(8,128)(2,1)} %param.12) | copy-start | bytes 393220
  163.8 1.3 copy-start.1
  309.0 3.3 copy-start.3
  309.0 15.1 %copy-start.4 = (f32[2048]{0:T(1024)S(1)}, f32[2048]{0:T(1024)}, u32[]{:S(2)}) copy-start(f32[2048]{0:T(1024)} %param.20) | copy-start | bytes 24580
  309.0 15.1 %copy-start.5 = (f32[2048]{0:T(1024)S(1)}, f32[2048]{0:T(1024)}, u32[]{:S(2)}) copy-start(f32[2048]{0:T(1024)} %param.19) | copy-start | bytes 24580
Sparse Core Ops, SparseCore 0:
  10.5 147.2 all-gather.7
  160.9 144.1 all-gather.9
  325.2 179.5 all-gather.11
where the time goes:
time: 1230 us; the launch traced here: 1220 us
  blocking collectives  720 us (59%)
  waiting for transfers between devices  337 us (27%)
  local copies, waits for them, and re-layouts  125 us (10%)
  between operations  14.6 us (1%)
  matrix products  12.3 us (1%)
    all_gather x4, blocking collectives, joined(): gathered = jax.tree.map(lambda a: lax.all_gather(a, axis), part)  581 us
    all_gather x1, waiting for transfers between devices, per_device(): lax.all_gather(normed, 'voc', axis=0, tiled=True)  180 us
    all_gather x1, waiting for transfers between devices, per_device(): lax.all_gather(mem_values, 'voc', axis=0, tiled=True)  139 us
    unnamed x1, blocking collectives  128 us
    dynamic_slice x130, local copies, waits for them, and re-layouts, take(): lax.dynamic_index_in_dim(a, source, 0, False)  110 us
  transfers between devices with their start and end apart: 3, of which 3 were waited for; matrix products, arithmetic and copies ran while one was open for 1% of the time, Pallas kernels for 0%

commit v1 on v0

v1 whole, which is shorter than its diff:
```python
import math

import jax
import jax.numpy as jnp
from jax import lax
from jax.experimental import pallas as pl
from jax.experimental.pallas import tpu as pltpu
from jax.sharding import Mesh
from jax.sharding import PartitionSpec as P

D = 2048
HEADS = 16
HEAD_DIM = D // HEADS

EPS_SMOOTH = 0.1
Z_COEF = 0.0001
LN_EPS = 1e-05

BF16 = jnp.bfloat16
F32 = jnp.float32

VOC = ("z", "yhi")


def attend_kernel(q_ref, r_ref, k_ref, v_ref, dec_ref, mem_ref, out_ref):
    scores = lax.dot_general(
        q_ref[...], k_ref[...], (((1,), (1,)), ((), ())), preferred_element_type=F32
    )
    scores = scores * (1.0 / math.sqrt(HEAD_DIM))
    scores = jnp.where(dec_ref[...] == mem_ref[...], scores, -jnp.inf)
    top = jnp.max(scores, axis=1, keepdims=True)
    raised = jnp.exp(scores - top)
    weights = (raised / jnp.sum(raised, axis=1, keepdims=True)).astype(BF16)
    context = jnp.dot(weights, v_ref[...], preferred_element_type=F32).astype(BF16)
    out_ref[...] = (r_ref[...].astype(F32) + context.astype(F32)).astype(BF16)


def attend(q, r, k, v, dec, mem):
    rows, mem_rows = q.shape[0], k.shape[0]
    tile = 128
    whole = lambda i: (0, 0)
    step = lambda i: (i, 0)
    return pl.pallas_call(
        attend_kernel,
        grid=(rows // tile,),
        in_specs=[
            pl.BlockSpec((tile, HEAD_DIM), step),
            pl.BlockSpec((tile, HEAD_DIM), step),
            pl.BlockSpec((mem_rows, HEAD_DIM), whole),
            pl.BlockSpec((mem_rows, HEAD_DIM), whole),
            pl.BlockSpec((tile, 1), step),
            pl.BlockSpec((1, mem_rows), whole),
        ],
        out_specs=pl.BlockSpec((tile, HEAD_DIM), step),
        out_shape=jax.ShapeDtypeStruct((rows, HEAD_DIM), BF16),
        compiler_params=pltpu.CompilerParams(vmem_limit_bytes=24 * 1024 * 1024),
        name="attend",
    )(q, r, k, v, dec, mem)


def head_kernel(vocab, starts_ref, x_ref, gain_ref, bias_ref, t_ref, w0_ref, w1_ref, out_ref, normed):
    heads, halves = x_ref.shape[0], x_ref.shape[2]
    chunk = x_ref.shape[-1]
    total = 0.0
    for half in range(halves):
        for head in range(heads):
            total = total + x_ref[head, 0, half].astype(F32)
    mean = jnp.sum(total, axis=1, keepdims=True) * (1.0 / D)
    square = 0.0
    for half in range(halves):
        for head in range(heads):
            centered = x_ref[head, 0, half].astype(F32) - mean
            square = square + centered * centered
    scale = lax.rsqrt(jnp.sum(square, axis=1, keepdims=True) * (1.0 / D) + LN_EPS)
    for half in range(halves):
        for head in range(heads):
            at = pl.ds((half * heads + head) * chunk, chunk)
            centered = x_ref[head, 0, half].astype(F32) - mean
            normed[:, at] = (centered * scale * gain_ref[:, at] + bias_ref[:, at]).astype(BF16)
    logits = [
        jnp.dot(normed[...], w_ref[...], preferred_element_type=F32) for w_ref in (w0_ref, w1_ref)
    ]
    top = jnp.maximum(
        jnp.max(logits[0], axis=1, keepdims=True), jnp.max(logits[1], axis=1, keepdims=True)
    )
    exps = sums = picks = 0.0
    for index, part in enumerate(logits):
        exps = exps + jnp.sum(jnp.exp(part - top), axis=1, keepdims=True)
        sums = sums + jnp.sum(part, axis=1, keepdims=True)
        column = lax.broadcasted_iota(jnp.int32, part.shape, 1) + starts_ref[index]
        picks = picks + jnp.sum(jnp.where(column == t_ref[...], part, 0.0), axis=1, keepdims=True)
    lse = top + jnp.log(exps)
    line = (1.0 - EPS_SMOOTH) * picks + (EPS_SMOOTH / vocab) * sums
    lane = lax.broadcasted_iota(jnp.int32, (lse.shape[0], 2), 1)
    out_ref[...] = jnp.where(lane == 0, lse, line)


def head_stats(x, gain, bias, targets, w0, w1, starts, vocab):
    heads, sets, halves, rows, chunk = x.shape
    tile = 128
    tiles = rows // tile
    whole = lambda i, s: (0, 0)
    spec = pltpu.PrefetchScalarGridSpec(
        num_scalar_prefetch=1,
        grid=(sets * tiles,),
        in_specs=[
            pl.BlockSpec(
                (heads, 1, halves, tile, chunk), lambda i, s: (0, i // tiles, 0, i % tiles, 0)
            ),
            pl.BlockSpec((1, D), whole),
            pl.BlockSpec((1, D), whole),
            pl.BlockSpec((tile, 1), lambda i, s: (i, 0)),
            pl.BlockSpec(w0.shape, whole),
            pl.BlockSpec(w1.shape, whole),
        ],
        out_specs=pl.BlockSpec((tile, 2), lambda i, s: (i, 0)),
        scratch_shapes=[pltpu.VMEM((tile, D), BF16)],
    )

    def kernel(*refs):
        head_kernel(vocab, *refs)

    return pl.pallas_call(
        kernel,
        grid_spec=spec,
        out_shape=jax.ShapeDtypeStruct((sets * rows, 2), F32),
        compiler_params=pltpu.CompilerParams(vmem_limit_bytes=40 * 1024 * 1024),
        name="head_stats",
    )(starts, x, gain, bias, targets, w0, w1)


def per_device(
    queries,
    residual,
    mem_keys,
    mem_values,
    dec_ids,
    mem_ids,
    targets,
    ln_gain,
    ln_bias,
    head_weight,
):
    enc, z, yhi = lax.axis_index("enc"), lax.axis_index("z"), lax.axis_index("yhi")
    z_count, y_count = lax.axis_size("z"), lax.axis_size("yhi")
    voc_count = z_count * y_count
    heads = queries.shape[1] // HEAD_DIM
    parts = voc_count // heads
    sets = parts // y_count
    rows, mem_rows = queries.shape[0], mem_keys.shape[0]
    piece = rows // parts
    width = head_weight.shape[1]
    vocab = width * voc_count * lax.axis_size("enc")

    with jax.named_scope("pack"):
        to_all = lambda a: jnp.broadcast_to(
            a.reshape(mem_rows, heads, 1, HEAD_DIM).transpose(1, 2, 0, 3),
            (heads, parts, mem_rows, HEAD_DIM),
        )
        to_part = lambda a: a.reshape(parts, piece, heads, HEAD_DIM).transpose(2, 0, 1, 3)
        dec_parts = dec_ids.reshape(parts, piece)
        target_sets = targets.reshape(sets, y_count, piece).transpose(1, 0, 2).reshape(y_count, -1)
        target_parts = jnp.broadcast_to(target_sets[None], (sets,) + target_sets.shape).reshape(
            parts, sets * piece
        )
        notes = jnp.concatenate(
            [
                dec_parts,
                jnp.broadcast_to(mem_ids[None], (parts, mem_rows)),
                target_parts // 256,
                target_parts % 256,
            ],
            axis=1,
        ).astype(BF16)
        notes = jnp.pad(notes, ((0, 0), (0, HEAD_DIM - notes.shape[1])))
        notes = jnp.broadcast_to(
            jnp.pad(notes[None, :, None], ((0, 0), (0, 0), (0, 7), (0, 0))),
            (heads, parts, 8, HEAD_DIM),
        )
        message = jnp.concatenate(
            [to_all(mem_keys), to_all(mem_values), to_part(queries), to_part(residual), notes],
            axis=2,
        ).reshape(voc_count, -1, HEAD_DIM)
    with jax.named_scope("spread"):
        got = lax.all_to_all(message, VOC, 0, 0, tiled=True)
    got, head_weight = lax.optimization_barrier((got, head_weight))
    with jax.named_scope("weights"):
        swap = [(0, 1), (1, 0)]
        weight_other = lax.ppermute(head_weight, "yhi", swap)

    with jax.named_scope("attention"):
        at_q = 2 * mem_rows
        take = lambda low, count: got[:, low : low + count].reshape(-1, HEAD_DIM)
        noted = got[:, at_q + 2 * piece].astype(jnp.int32)
        dec = noted[:, :piece].reshape(-1, 1)
        mem = noted[:, piece : piece + mem_rows].reshape(1, -1)
        at_t = piece + mem_rows
        target = (
            noted[:, at_t : at_t + sets * piece] * 256
            + noted[:, at_t + sets * piece : at_t + 2 * sets * piece]
        )
        target = target.reshape(voc_count, sets, piece).transpose(1, 0, 2).reshape(-1, 1)
        summed = attend(
            take(at_q, piece),
            take(at_q + piece, piece),
            take(0, mem_rows),
            take(mem_rows, mem_rows),
            dec,
            mem,
        )
    with jax.named_scope("rows"):
        full = lax.all_gather(summed, ("z", "enc"), axis=0)
        full = full.reshape((heads, sets, lax.axis_size("enc")) + summed.shape)
    with jax.named_scope("head"):
        slab = (enc * voc_count + z * y_count) * width
        starts = jnp.stack([slab + yhi * width, slab + (1 - yhi) * width]).astype(jnp.int32)
        stats = head_stats(
            full,
            ln_gain[None],
            ln_bias[None],
            target,
            head_weight,
            weight_other,
            starts,
            vocab,
        )
    with jax.named_scope("merge"):
        enc_count = lax.axis_size("enc")
        stats = stats.reshape(sets, voc_count, piece, 2).transpose(1, 3, 0, 2)
        stats = stats.reshape(voc_count, 2, sets * piece)
        stats = jnp.broadcast_to(stats[None], (enc_count,) + stats.shape)
        stats = stats.reshape(enc_count * voc_count, 2, sets * piece)
        merged = lax.all_to_all(stats, ("enc",) + VOC, 0, 0, tiled=True)
        merged = merged.reshape(enc_count * z_count, y_count, 2, sets * piece)
        lse, line = merged[:, :, 0], merged[:, :, 1]
        top = jnp.max(lse, axis=0)
        log_total = top + jnp.log(jnp.sum(jnp.exp(lse - top), axis=0))
        loss = log_total - jnp.sum(line, axis=0) + Z_COEF * log_total * log_total
        return loss.reshape(y_count, sets, piece).transpose(1, 0, 2).reshape(rows)


def solution(mesh):
    shape = dict(mesh.shape)
    fine = Mesh(
        mesh.devices.reshape(shape["enc"], shape["blk"], shape["voc"] // 2, 2),
        ("enc", "blk", "z", "yhi"),
    )
    held = ("blk",) + VOC
    in_specs = (
        P(held, "enc"),
        P(held, "enc"),
        P(held, "enc"),
        P(held, "enc"),
        P(held),
        P(held),
        P(held),
        P(),
        P(),
        P(None, ("enc",) + VOC),
    )
    return jax.shard_map(
        per_device, mesh=fine, in_specs=in_specs, out_specs=P(held), check_vma=False
    )
```

time: 1230 us -> 198 us (0.16)
  blocking collectives: 720 us -> 90.6 us
  waiting for transfers between devices: 337 us -> 62.1 us
  local copies, waits for them, and re-layouts: 125 us -> 8.93 us
  Pallas kernels: 0 us -> 16 us
  matrix products: 12.3 us -> 0 us
    all_gather x5 -> x0, blocking collectives: 592 us -> none  [the longest x4 581 us: joined(): gathered = jax.tree.map(lambda a: lax.all_gather(a, axis), part)]
    all_gather x3 -> x1, waiting for transfers between devices: 336 us -> 18.6 us  [per_device(): full = lax.all_gather(summed, ('z', 'enc'), axis=0)]
    unnamed x1 -> x0, blocking collectives: 128 us -> none
    dynamic_slice x130 -> x0, local copies, waits for them, and re-layouts: 110 us -> none  [take(): lax.dynamic_index_in_dim(a, source, 0, False)]
    all_to_all x0 -> x2, blocking collectives: none -> 90.6 us  [the longest x1 64 us: per_device(): got = lax.all_to_all(message, VOC, 0, 0, tiled=True)]
    ppermute x0 -> x1, waiting for transfers between devices: none -> 43.4 us  [per_device(): weight_other = lax.ppermute(head_weight, 'yhi', swap)]
    pallas_call x0 -> x2, Pallas kernels: none -> 16 us  [the longest x1 12.8 us: head_stats(): pl.pallas_call(kernel, grid_spec=spec, out_shape=jax.ShapeDtypeStruct((se...]
  transfers between devices with their start and end apart: 3 -> 2, of which waited for: 3 -> 2; matrix products, arithmetic and copies ran while one was open for 1% -> 0% of each run, Pallas kernels for 0% -> 0%
where the time goes in v1:
time: 198 us
  blocking collectives  90.6 us (46%)
  waiting for transfers between devices  62.1 us (31%)
  Pallas kernels  16 us (8%)
  between operations  13.6 us (7%)
  local copies, waits for them, and re-layouts  8.93 us (5%)
  starting transfers between devices  5.05 us (3%)
    all_to_all x1, blocking collectives, per_device(): got = lax.all_to_all(message, VOC, 0, 0, tiled=True)  64 us
    ppermute x1, waiting for transfers between devices, per_device(): weight_other = lax.ppermute(head_weight, 'yhi', swap)  43.4 us
    all_to_all x1, blocking collectives, per_device(): merged = lax.all_to_all(stats, ('enc',) + VOC, 0, 0, tiled=True)  26.6 us
    all_gather x1, waiting for transfers between devices, per_device(): full = lax.all_gather(summed, ('z', 'enc'), axis=0)  18.6 us
    pallas_call x1, Pallas kernels, head_stats(): pl.pallas_call(kernel, grid_spec=spec, out_shape=jax.ShapeDtypeStruct((se...  12.8 us
    unnamed x16, local copies, waits for them, and re-layouts  5.92 us
    ppermute x1, starting transfers between devices, per_device(): weight_other = lax.ppermute(head_weight, 'yhi', swap)  5.04 us
  transfers between devices with their start and end apart: 2, of which 2 were waited for; matrix products, arithmetic and copies ran while one was open for 0% of the time, Pallas kernels for 0%

profile of v1, /device:TPU:1, one launch (start us, length us, event | category | flops | bytes accessed | tf_op | source)
XLA Modules:
  0.0 197.9 jit_solution(12193685812594207959)
XLA Ops:
  6.5 0.0 all-gather.3.cloned.1.call-start
  6.5 0.7 convert.15
  7.2 0.1 reshape.82
  7.3 0.7 convert.16
  7.9 0.7 reshape.83
  8.7 0.1 broadcast_in_dim.56
  8.8 0.1 pad.11.clone
  8.9 0.1 pad_maximum_fusion
  9.0 0.9 copy.110
  9.8 0.9 copy.111
  10.7 0.9 copy.112
  11.7 0.9 copy.113
  12.7 0.1 broadcast_dynamic-update-slice_fusion
  12.8 0.0 copy-start.1
  12.8 64.0 %all_to_all.10 = bf16[32,104,128]{2,1,0:T(8,128)(2,1)S(1)} all-to-all(bf16[32,104,128]{2,1,0:T(8,128)(2,1)S(1)} %bitcast.75), channel_id=1, replica_groups=mesh['enc'=2,'blk'=8,'z'=16,'yhi'=2] {'z','yhi'}, dimensions={0} | all-to-all | bytes 1703936 | tf_op jit(solution)/shard_map/spread/all_to_all | solution.py:185
  76.9 0.0 copy-start.2
  76.9 0.0 copy-start.3
  76.9 0.1 slice_add_fusion
  77.0 0.1 reshape.91.mem_ref
  77.1 0.2 reshape.102.dec_ref
  77.3 3.1 %attend.1 = bf16[512,128]{1,0:T(8,128)(2,1)} custom-call(bf16[512,128]{1,0:T(8,128)(2,1)S(1)} %bitcast.72, bf16[512,128]{1,0:T(8,128)(2,1)S(1)} %bitcast.71, bf16[1024,128]{1,0:T(8,128)(2,1)S(1)} %bitcast.70, bf16[1024,128]{1,0:T(8,128)(2,1)S(1)} %bitcast.69, s32[512,1]{1,0:T(8,128)S(1)} %reshape.102.dec_ref, s32[1,1024]{1,0:T(1,128)S(1)} %reshape.91.mem_ref), custom_call_target="tpu_custom_call" | custom-call | tf_op jit(solution)/shard_map/attention/attend/pallas_call | solution.py:43
  80.4 0.0 all-gather.3.cloned.1.call-update
  80.4 0.0 copy-done.1
  80.4 5.0 %collective-permute-start = (bf16[2048,512]{1,0:T(8,128)(2,1)S(1)}, bf16[2048,512]{1,0:T(8,128)(2,1)}, u32[]{:S(2)}, u32[]{:S(2)}) collective-permute-start(bf16[2048,512]{1,0:T(8,128)(2,1)S(1)} %copy-done.1), channel_id=1, source_target_pairs={{0,1},{1,0},{2,3},{3,2},{4,5},{5,4},{6,7},{7,6},{8,9},{9,8},{10,11... | collective-permute-start | bytes 6291464 | tf_op jit(solution)/shard_map/weights/ppermute | solution.py:189
  85.5 0.1 pad_add_fusion.refs_0_
  85.6 0.1 copy.97
  85.6 0.1 copy.98
  85.7 0.3 reshape.103.refs_4_
  86.0 43.4 %collective-permute-done.refs_6_ = bf16[2048,512]{1,0:T(8,128)(2,1)} collective-permute-done((bf16[2048,512]{1,0:T(8,128)(2,1)S(1)}, bf16[2048,512]{1,0:T(8,128)(2,1)}, u32[]{:S(2)}, u32[]{:S(2)}) %collective-permute-start) | collective-permute-done | bytes 2097184 | tf_op jit(solution)/shard_map/weights/ppermute | solution.py:189
  129.5 18.6 %all-gather.3.cloned.1.call-done = bf16[16384,128]{1,0:T(8,128)(2,1)} async-done(((bf16[512,128]{1,0:T(8,128)(2,1)}), bf16[16384,128]{1,0:T(8,128)(2,1)}) %all-gather.3.cloned.1.call-update) | async-done | bytes 4194320 | tf_op jit(solution)/shard_map/rows/all_gather | solution.py:212
  148.1 0.0 copy-done.2
  148.1 0.0 copy-done.3
  148.1 0.0 copy-start
  148.1 2.2 %copy-done = bf16[16384,128]{1,0:T(8,128)(2,1)S(1)} copy-done((bf16[16384,128]{1,0:T(8,128)(2,1)S(1)}, bf16[16384,128]{1,0:T(8,128)(2,1)}, u32[]{:S(2)}) %copy-start) | copy-done | bytes 4194328
  150.3 12.8 %head_stats.1 = f32[1024,2]{1,0:T(8,128)S(1)} custom-call(s32[2]{0:T(128)S(1)} %pad_add_fusion.refs_0_, bf16[8,2,2,512,128]{4,3,2,1,0:T(8,128)(2,1)S(1)} %bitcast.67, f32[1,2048]{1,0:T(1,128)S(1)} %bitcast.73, f32[1,2048]{1,0:T(1,128)S(1)} %bitcast.74, s32[1024,1]{1,0:T(8,128)S(1)} %reshape.103.refs_4_, bf16[2048,512]{1,0:T(8,128)(2,1)S(1)} %copy-done.1, ...), custom_call_target="tpu_custom_call" | custom-call | tf_op jit(solution)/shard_map/head/head_stats/pallas_call | solution.py:123
  163.1 0.3 copy.100
  163.4 0.1 copy.101
  163.5 26.6 %all_to_all.11 = f32[64,2,32]{2,1,0:T(2,128)S(1)} all-to-all(f32[64,2,32]{2,1,0:T(2,128)S(1)} %bitcast.84), channel_id=1, replica_groups=mesh['enc'=2,'blk'=8,'z'=16,'yhi'=2] {'enc','z','yhi'}, dimensions={0} | all-to-all | bytes 32768 | tf_op jit(solution)/shard_map/merge/all_to_all | solution.py:233
  190.2 0.1 fusion.1
  190.2 0.1 add.40
  190.3 0.1 reduce_sum.22
  190.4 0.6 reshape.98
  (23 shorter events, 0.4 us)
Async XLA Ops:
  6.5 141.6 %all-gather.3.cloned.1.call-start = ((), (), s32[]{:S(2)}) async-start(), calls=%async_computation.2 | async-start | bytes 4325376 | tf_op jit(solution)/shard_map/rows/all_gather | solution.py:212
  12.8 67.6 %copy-start.1 = (bf16[2048,512]{1,0:T(8,128)(2,1)S(1)}, bf16[2048,512]{1,0:T(8,128)(2,1)}, u32[]{:S(2)}) copy-start(bf16[2048,512]{1,0:T(8,128)(2,1)} %refs_5_) | copy-start | bytes 6291460
  76.9 71.2 %copy-start.2 = (f32[2048]{0:T(1024)S(1)}, f32[2048]{0:T(1024)}, u32[]{:S(2)}) copy-start(f32[2048]{0:T(1024)} %param.17) | copy-start | bytes 24580
  76.9 71.2 %copy-start.3 = (f32[2048]{0:T(1024)S(1)}, f32[2048]{0:T(1024)}, u32[]{:S(2)}) copy-start(f32[2048]{0:T(1024)} %param.18) | copy-start | bytes 24580
  80.4 49.0 %collective-permute-start = (bf16[2048,512]{1,0:T(8,128)(2,1)S(1)}, bf16[2048,512]{1,0:T(8,128)(2,1)}, u32[]{:S(2)}, u32[]{:S(2)}) collective-permute-start(bf16[2048,512]{1,0:T(8,128)(2,1)S(1)} %copy-done.1), channel_id=1, source_target_pairs={{0,1},{1,0},{2,3},{3,2},{4,5},{5,4},{6,7},{7,6},{8,9},{9,8},{10,11... | collective-permute-start | bytes 6291464 | tf_op jit(solution)/shard_map/weights/ppermute | solution.py:189
  148.1 2.2 %copy-start = (bf16[16384,128]{1,0:T(8,128)(2,1)S(1)}, bf16[16384,128]{1,0:T(8,128)(2,1)}, u32[]{:S(2)}) copy-start(bf16[16384,128]{1,0:T(8,128)(2,1)} %all-gather.3.cloned.1.call-done) | copy-start | bytes 12582916
Sparse Core Ops, SparseCore 0:
  80.5 67.4 all-gather.2

commit v2 on v1

v2 whole, which is shorter than its diff:
```python
import math

import jax
import jax.numpy as jnp
from jax import lax
from jax.experimental import pallas as pl
from jax.experimental.pallas import tpu as pltpu
from jax.sharding import Mesh
from jax.sharding import PartitionSpec as P

D = 2048
HEADS = 16
HEAD_DIM = D // HEADS

EPS_SMOOTH = 0.1
Z_COEF = 0.0001
LN_EPS = 1e-05

BF16 = jnp.bfloat16
F32 = jnp.float32
MIB = 1024 * 1024

VOC = ("z", "yhi")
SWAP = [(0, 1), (1, 0)]
EARLY_SHARE = 14 / 32


def pack_kernel(parts, q_ref, r_ref, k_ref, v_ref, out_ref):
    mem_rows = k_ref.shape[0]
    piece = q_ref.shape[0] // parts
    at_q = 2 * mem_rows
    for head in range(q_ref.shape[1] // HEAD_DIM):
        lanes = pl.ds(head * HEAD_DIM, HEAD_DIM)
        for part in range(parts):
            to = head * parts + part
            rows = pl.ds(part * piece, piece)
            out_ref[to, pl.ds(0, mem_rows)] = k_ref[:, lanes]
            out_ref[to, pl.ds(mem_rows, mem_rows)] = v_ref[:, lanes]
            out_ref[to, pl.ds(at_q, piece)] = q_ref[rows, lanes]
            out_ref[to, pl.ds(at_q + piece, piece)] = r_ref[rows, lanes]


def pack(q, r, k, v, parts):
    heads = q.shape[1] // HEAD_DIM
    depth = 2 * k.shape[0] + 2 * (q.shape[0] // parts)

    def kernel(*refs):
        pack_kernel(parts, *refs)

    return pl.pallas_call(
        kernel,
        out_shape=jax.ShapeDtypeStruct((heads * parts, depth, HEAD_DIM), BF16),
        compiler_params=pltpu.CompilerParams(vmem_limit_bytes=16 * MIB),
        name="pack",
    )(q, r, k, v)


def attend_kernel(piece, q_ref, r_ref, k_ref, v_ref, dec_ref, mem_ref, out_ref):
    scores = lax.dot_general(
        q_ref[...], k_ref[...], (((1,), (1,)), ((), ())), preferred_element_type=F32
    )
    scores = scores * (1.0 / math.sqrt(HEAD_DIM))
    scores = jnp.where(dec_ref[...] == mem_ref[...], scores, -jnp.inf)
    top = jnp.max(scores, axis=1, keepdims=True)
    raised = jnp.exp(scores - top)
    weights = (raised / jnp.sum(raised, axis=1, keepdims=True)).astype(BF16)
    context = jnp.dot(weights, v_ref[...], preferred_element_type=F32).astype(BF16)
    summed = r_ref[...].astype(F32) + context.astype(F32)
    halves = out_ref.shape[0]
    summed = summed.reshape(-1, halves, piece // halves, HEAD_DIM)
    for half in range(halves):
        out_ref[half] = summed[:, half].reshape(-1, HEAD_DIM).astype(BF16)


def attend(q, r, k, v, dec, mem, piece, halves):
    rows, mem_rows = q.shape[0], k.shape[0]
    tile = 128
    whole = lambda i: (0, 0)
    step = lambda i: (i, 0)

    def kernel(*refs):
        attend_kernel(piece, *refs)

    return pl.pallas_call(
        kernel,
        grid=(rows // tile,),
        in_specs=[
            pl.BlockSpec((tile, HEAD_DIM), step),
            pl.BlockSpec((tile, HEAD_DIM), step),
            pl.BlockSpec((mem_rows, HEAD_DIM), whole),
            pl.BlockSpec((mem_rows, HEAD_DIM), whole),
            pl.BlockSpec((tile, 1), step),
            pl.BlockSpec((1, mem_rows), whole),
        ],
        out_specs=pl.BlockSpec((halves, tile // halves, HEAD_DIM), lambda i: (0, i, 0)),
        out_shape=jax.ShapeDtypeStruct((halves, rows // halves, HEAD_DIM), BF16),
        compiler_params=pltpu.CompilerParams(vmem_limit_bytes=24 * MIB),
        name="attend",
    )(q, r, k, v, dec, mem)


def head_kernel(vocab, info_ref, x_ref, gain_ref, bias_ref, t_ref, *rest):
    slabs = len(rest) - 5
    w_refs = rest[:slabs]
    out_ref, held, normed, logits, sems = rest[slabs:]
    copies = [
        pltpu.make_async_copy(w_refs[k], held.at[k], sems.at[k]) for k in range(slabs)
    ]
    for copy in copies:
        copy.start()
    heads, sets, halves, rows, chunk = x_ref.shape
    mine = info_ref[slabs]
    step = 16
    for group in range(sets):
        for low in range(0, rows, step):
            at = pl.ds(low, step)
            parts = [
                x_ref[head, group, half, at].astype(F32)
                for half in range(halves)
                for head in range(heads)
            ]
            mean = jnp.sum(sum(parts[1:], parts[0]), axis=1, keepdims=True) * (1.0 / D)
            parts = [part - mean for part in parts]
            squares = [part * part for part in parts]
            var = jnp.sum(sum(squares[1:], squares[0]), axis=1, keepdims=True) * (1.0 / D)
            scale = lax.rsqrt(var + LN_EPS)
            for half in range(halves):
                base = jnp.where(mine == 0, half, 1 - half) * (heads * chunk)
                for head in range(heads):
                    lanes = pl.ds(pl.multiple_of(base + head * chunk, chunk), chunk)
                    value = parts[half * heads + head] * scale * gain_ref[:, lanes]
                    normed[pl.ds(group * rows + low, step), lanes] = (
                        value + bias_ref[:, lanes]
                    ).astype(BF16)
    total = sets * rows
    width = held.shape[2]
    for k in range(slabs):
        copies[k].wait()
        logits[:, pl.ds(k * width, width)] = jnp.dot(
            normed[...], held[k], preferred_element_type=F32
        )
    lane = lax.broadcasted_iota(jnp.int32, (step, 128), 1)
    for low in range(0, total, step):
        at = pl.ds(low, step)
        target = t_ref[at]
        top = logits[at, pl.ds(0, 128)]
        for col in range(128, slabs * width, 128):
            top = jnp.maximum(top, logits[at, pl.ds(col, 128)])
        top = jnp.max(top, axis=1, keepdims=True)
        exps = sums = picks = jnp.zeros((step, 128), F32)
        for k in range(slabs):
            offset = target - info_ref[k]
            for col in range(0, width, 128):
                part = logits[at, pl.ds(k * width + col, 128)]
                exps = exps + jnp.exp(part - top)
                sums = sums + part
                picks = picks + jnp.where(lane == offset - col, part, 0.0)
        lse = top + jnp.log(jnp.sum(exps, axis=1, keepdims=True))
        line = (1.0 - EPS_SMOOTH) * picks + (EPS_SMOOTH / vocab) * sums
        line = jnp.sum(line, axis=1, keepdims=True)
        pair = lax.broadcasted_iota(jnp.int32, (step, 2), 1)
        out_ref[at] = jnp.where(pair == 0, lse, line)


def head_stats(x, gain, bias, targets, slabs, info, vocab):
    heads, sets, halves, rows, chunk = x.shape
    total = sets * rows
    width = slabs[0].shape[1]

    def kernel(*refs):
        head_kernel(vocab, *refs)

    vmem = pl.BlockSpec(memory_space=pltpu.VMEM)
    return pl.pallas_call(
        kernel,
        in_specs=[pl.BlockSpec(memory_space=pltpu.SMEM), vmem, vmem, vmem, vmem]
        + [pl.BlockSpec(memory_space=pl.ANY)] * len(slabs),
        out_specs=vmem,
        out_shape=jax.ShapeDtypeStruct((total, 2), F32),
        scratch_shapes=[
            pltpu.VMEM((len(slabs), D, width), BF16),
            pltpu.VMEM((total, D), BF16),
            pltpu.VMEM((total, len(slabs) * width), F32),
            pltpu.SemaphoreType.DMA((len(slabs),)),
        ],
        compiler_params=pltpu.CompilerParams(vmem_limit_bytes=40 * MIB),
        name="head_stats",
    )(info, x, gain, bias, targets, *slabs)


def per_device(
    queries,
    residual,
    mem_keys,
    mem_values,
    dec_ids,
    mem_ids,
    targets,
    ln_gain,
    ln_bias,
    head_weight,
):
    enc, z, yhi = lax.axis_index("enc"), lax.axis_index("z"), lax.axis_index("yhi")
    enc_count, z_count, y_count = (lax.axis_size(name) for name in ("enc", "z", "yhi"))
    voc_count = z_count * y_count
    heads = queries.shape[1] // HEAD_DIM
    parts = voc_count // heads
    sets = parts // y_count
    rows, mem_rows = queries.shape[0], mem_keys.shape[0]
    piece = rows // parts
    slice_rows = piece // enc_count
    width = head_weight.shape[1]
    vocab = width * voc_count * enc_count

    with jax.named_scope("pack"):
        message = pack(queries, residual, mem_keys, mem_values, parts)
        first = jnp.concatenate([dec_ids, mem_ids, jnp.zeros((128 - rows - mem_rows,), jnp.int32)])
        second = jnp.concatenate([targets // 256, targets % 256])
        notes = jnp.stack([first, second]).astype(BF16)
        notes = jnp.broadcast_to(jnp.pad(notes, ((0, 6), (0, 0)))[None], (voc_count, 8, HEAD_DIM))
        message = jnp.concatenate([message, notes], axis=1)
    with jax.named_scope("spread"):
        got = lax.all_to_all(message, VOC, 0, 0, tiled=True)
    got, head_weight = lax.optimization_barrier((got, head_weight))
    with jax.named_scope("weights"):
        weight_y = lax.ppermute(head_weight, "yhi", SWAP)
        weight_e = lax.ppermute(head_weight, "enc", SWAP)
        weight_ye = lax.ppermute(weight_y, "enc", SWAP)

    with jax.named_scope("attention"):
        at_q = 2 * mem_rows
        take = lambda low, count: got[:, low : low + count].reshape(-1, HEAD_DIM)
        noted = got[:, at_q + 2 * piece : at_q + 2 * piece + 2].astype(jnp.int32)
        dec = lax.dynamic_slice_in_dim(
            noted[:, 0], ((z % sets) * y_count + yhi) * piece, piece, 1
        ).reshape(-1, 1)
        mem = noted[:, 0, rows : rows + mem_rows].reshape(1, -1)
        target = noted[:, 1, :rows] * 256 + noted[:, 1, rows:]
        target = target.reshape(voc_count, sets, y_count * enc_count, slice_rows)
        target = lax.dynamic_index_in_dim(target, yhi * enc_count + enc, 2, False)
        target = target.transpose(1, 0, 2)
        halves = attend(
            take(at_q, piece),
            take(at_q + piece, piece),
            take(0, mem_rows),
            take(mem_rows, mem_rows),
            dec,
            mem,
            piece,
            enc_count,
        )
    with jax.named_scope("halves"):
        kept = lax.dynamic_index_in_dim(halves, enc, 0, False)
        handed = lax.ppermute(
            lax.dynamic_index_in_dim(halves, 1 - enc, 0, False), "enc", SWAP
        )
        shard = jnp.stack([kept, handed])
    early = int(voc_count * EARLY_SHARE)
    slab = lambda e, y: ((e * voc_count) + z * y_count + y) * width
    info = jnp.stack(
        [slab(enc, yhi), slab(1 - enc, yhi), slab(enc, 1 - yhi), slab(1 - enc, 1 - yhi), enc]
    ).astype(jnp.int32)
    found = []
    for low, high in ((early, voc_count), (0, early)):
        with jax.named_scope("rows"):
            full = lax.all_gather(shard[:, low * slice_rows : high * slice_rows], "z", axis=0)
            full = full.reshape((heads, sets) + full.shape[1:])
        with jax.named_scope("head"):
            stats = head_stats(
                full,
                ln_gain[None],
                ln_bias[None],
                target[:, low:high].reshape(-1, 1),
                (head_weight, weight_e, weight_y, weight_ye),
                info,
                vocab,
            )
            found.append(stats.reshape(sets, high - low, slice_rows, 2))
    with jax.named_scope("merge"):
        stats = jnp.concatenate(found[::-1], axis=1).transpose(1, 3, 0, 2)
        stats = jnp.broadcast_to(
            stats.reshape(1, voc_count, 2, -1), (enc_count, voc_count, 2, sets * slice_rows)
        )
        merged = lax.all_to_all(
            stats.reshape(enc_count * voc_count, 2, -1), ("enc",) + VOC, 0, 0, tiled=True
        )
        merged = merged.reshape(enc_count, z_count, y_count, 2, sets, slice_rows)
        lse, line = merged[:, :, :, 0], merged[:, :, :, 1]
        top = jnp.max(lse, axis=1, keepdims=True)
        log_total = top[:, 0] + jnp.log(jnp.sum(jnp.exp(lse - top), axis=1))
        loss = log_total - jnp.sum(line, axis=1) + Z_COEF * log_total * log_total
        return loss.transpose(2, 1, 0, 3).reshape(rows)


def solution(mesh):
    shape = dict(mesh.shape)
    fine = Mesh(
        mesh.devices.reshape(shape["enc"], shape["blk"], shape["voc"] // 2, 2),
        ("enc", "blk", "z", "yhi"),
    )
    held = ("blk",) + VOC
    in_specs = (
        P(held, "enc"),
        P(held, "enc"),
        P(held, "enc"),
        P(held, "enc"),
        P(held),
        P(held),
        P(held),
        P(),
        P(),
        P(None, ("enc",) + VOC),
    )
    return jax.shard_map(
        per_device, mesh=fine, in_specs=in_specs, out_specs=P(held), check_vma=False
    )
```

time: 198 us -> 209 us (1.056)
  blocking collectives: 90.6 us -> 121 us
  waiting for transfers between devices: 62.1 us -> 34.7 us
  starting transfers between devices: 5.05 us -> 15 us
    all_gather x0 -> x1, blocking collectives: none -> 28.6 us  [per_device(): lax.all_gather(shard[:, low * slice_rows:high * slice_rows], 'z', axis=0)]
    all_gather x1, waiting for transfers between devices: 18.6 us -> 0.01 us  [per_device(): lax.all_gather(shard[:, low * slice_rows:high * slice_rows], 'z', axis=0)]
    ppermute x1 -> x4, starting transfers between devices: 5.04 us -> 15 us  [the longest x1 5.06 us: per_device(): weight_y = lax.ppermute(head_weight, 'yhi', SWAP)]
    ppermute x1 -> x4, waiting for transfers between devices: 43.4 us -> 34.7 us  [the longest x1 33.8 us: per_device(): weight_y = lax.ppermute(head_weight, 'yhi', SWAP)]
    pallas_call x2 -> x4, Pallas kernels: 16 us -> 14.4 us  [the longest x2 11.8 us: head_stats(): pl.pallas_call(kernel, in_specs=[pl.BlockSpec(memory_space=pltpu.SMEM), v...]
  transfers between devices with their start and end apart: 2 -> 5, of which waited for: 2 -> 2; matrix products, arithmetic and copies ran while one was open for 0% -> 1% of each run, Pallas kernels for 0% -> 4%
where the time goes in v2:
time: 209 us
  blocking collectives  121 us (58%)
  waiting for transfers between devices  34.7 us (17%)
  starting transfers between devices  15 us (7%)
  Pallas kernels  14.4 us (7%)
  between operations  13.7 us (7%)
  local copies, waits for them, and re-layouts  7.21 us (3%)
  other arithmetic  3.1 us (1%)
    all_to_all x1, blocking collectives, per_device(): got = lax.all_to_all(message, VOC, 0, 0, tiled=True)  64 us
    ppermute x1, waiting for transfers between devices, per_device(): weight_y = lax.ppermute(head_weight, 'yhi', SWAP)  33.8 us
    all_gather x1, blocking collectives, per_device(): lax.all_gather(shard[:, low * slice_rows:high * slice_rows], 'z', axis=0)  28.6 us
    all_to_all x1, blocking collectives, per_device(): lax.all_to_all(stats.reshape(enc_count * voc_count, 2, -1), ('enc',) + VO...  28.1 us
    pallas_call x2, Pallas kernels, head_stats(): pl.pallas_call(kernel, in_specs=[pl.BlockSpec(memory_space=pltpu.SMEM), v...  11.8 us
    ppermute x1, starting transfers between devices, per_device(): weight_y = lax.ppermute(head_weight, 'yhi', SWAP)  5.06 us
    unnamed x16, local copies, waits for them, and re-layouts  4.76 us
    ppermute x1, starting transfers between devices, per_device(): weight_ye = lax.ppermute(weight_y, 'enc', SWAP)  4.58 us
  transfers between devices with their start and end apart: 5, of which 2 were waited for; matrix products, arithmetic and copies ran while one was open for 1% of the time, Pallas kernels for 4%

profile of v2, /device:TPU:1, one launch (start us, length us, event | category | flops | bytes accessed | tf_op | source)
XLA Modules:
  0.0 208.9 jit_solution(3129146913448579795)
XLA Ops:
  6.5 0.7 fusion.7
  7.2 0.7 convert.18
  7.9 0.7 convert.19
  8.5 0.1 maximum_bitcast_fusion.1
  8.6 0.0 copy-start.2
  8.6 0.9 copy-done.2
  9.5 0.9 copy-done.3
  10.4 0.8 copy-done.4
  11.3 0.8 copy-done.5
  12.1 0.1 pack.1
  12.2 0.1 pad_maximum_fusion
  12.3 64.0 %all_to_all.10 = bf16[32,104,128]{2,1,0:T(8,128)(2,1)S(1)} all-to-all(bf16[32,104,128]{2,1,0:T(8,128)(2,1)S(1)} %pad_maximum_fusion), channel_id=1, replica_groups=mesh['enc'=2,'blk'=8,'z'=16,'yhi'=2] {'z','yhi'}, dimensions={0} | all-to-all | bytes 1703936 | tf_op jit(solution)/shard_map/spread/all_to_all | solution.py:223
  76.3 5.1 %collective-permute-start.2 = (bf16[2048,512]{1,0:T(8,128)(2,1)S(1)}, bf16[2048,512]{1,0:T(8,128)(2,1)}, u32[]{:S(2)}, u32[]{:S(2)}) collective-permute-start(bf16[2048,512]{1,0:T(8,128)(2,1)S(1)} %copy-done), channel_id=1, source_target_pairs={{0,1},{1,0},{2,3},{3,2},{4,5},{5,4},{6,7},{7,6},{8,9},{9,8},{10,11... | collective-permute-start | bytes 6291464 | tf_op jit(solution)/shard_map/weights/ppermute | solution.py:226
  81.4 0.1 dynamic-slice_reduce_fusion
  81.6 0.2 reshape.72.refs_4_
  81.7 0.1 slice_reduce_fusion.2
  81.9 0.1 squeeze.19.refs_5_
  82.0 0.0 copy-start.6
  82.0 0.0 copy-start.7
  82.0 2.5 %attend.1 = bf16[2,256,128]{2,1,0:T(8,128)(2,1)S(1)} custom-call(bf16[512,128]{1,0:T(8,128)(2,1)S(1)} %bitcast.54, bf16[512,128]{1,0:T(8,128)(2,1)S(1)} %bitcast.53, bf16[1024,128]{1,0:T(8,128)(2,1)S(1)} %bitcast.51, bf16[1024,128]{1,0:T(8,128)(2,1)S(1)} %bitcast.50, s32[512,1]{1,0:T(8,128)S(1)} %reshape.72.refs_4_, s32[1,1024]{1,0:T(1,128)S(1)} %squeeze.19.refs_5_), custom_call_target="tpu_custom_call" | custom-call | tf_op jit(solution)/shard_map/attention/attend/pallas_call | solution.py:84
  84.6 3.1 %collective-permute-start = (bf16[256,128]{1,0:T(8,128)(2,1)S(1)}, bf16[256,128]{1,0:T(8,128)(2,1)S(1)}, u32[]{:S(2)}, u32[]{:S(2)}) collective-permute-start(bf16[256,128]{1,0:T(8,128)(2,1)S(1)} %get-tuple-element.16), channel_id=1, source_target_pairs={{0,256},{256,0},{1,257},{257,1},{2,258},{258,2},{3,259},{259,3},{4... | collective-permute-start | bytes 196616 | tf_op jit(solution)/shard_map/halves/ppermute | solution.py:254
  87.7 0.9 collective-permute-done
  88.6 0.6 pad_maximum_fusion.1
  89.2 0.0 all-gather.4.cloned.1.call-update
  89.3 2.3 %collective-permute-start.1 = (bf16[2048,512]{1,0:T(8,128)(2,1)S(1)}, bf16[2048,512]{1,0:T(8,128)(2,1)}, u32[]{:S(2)}, u32[]{:S(2)}) collective-permute-start(bf16[2048,512]{1,0:T(8,128)(2,1)S(1)} %copy-done), channel_id=1, source_target_pairs={{0,256},{256,0},{1,257},{257,1},{2,258},{258,2},{3,259},{259,3},{4... | collective-permute-start | bytes 6291464 | tf_op jit(solution)/shard_map/weights/ppermute | solution.py:227
  91.5 33.8 %collective-permute-done.2.refs_7_ = bf16[2048,512]{1,0:T(8,128)(2,1)} collective-permute-done((bf16[2048,512]{1,0:T(8,128)(2,1)S(1)}, bf16[2048,512]{1,0:T(8,128)(2,1)}, u32[]{:S(2)}, u32[]{:S(2)}) %collective-permute-start.2) | collective-permute-done | bytes 2097184 | tf_op jit(solution)/shard_map/weights/ppermute | solution.py:226
  125.4 4.6 %collective-permute-start.3 = (bf16[2048,512]{1,0:T(8,128)(2,1)}, bf16[2048,512]{1,0:T(8,128)(2,1)}, u32[]{:S(2)}, u32[]{:S(2)}) collective-permute-start(bf16[2048,512]{1,0:T(8,128)(2,1)} %collective-permute-done.2.refs_7_), channel_id=1, source_target_pairs={{0,256},{256,0},{1,257},{257,1},{2,258},{258,2},{3,259},{259,3},{4... | collective-permute-start | bytes 6291464 | tf_op jit(solution)/shard_map/weights/ppermute | solution.py:228
  130.0 0.1 stack.42.refs_0_
  130.1 0.1 slice_add_fusion
  130.2 0.1 copy.44
  130.3 0.1 slice.65
  130.3 0.1 copy.45
  130.4 0.1 reshape.73.refs_4_
  130.5 0.1 copy.47
  130.6 0.1 reshape.74.refs_4_
  130.7 28.6 %all-gather = bf16[32,112,128]{2,1,0:T(8,128)(2,1)S(1)} all-gather(bf16[2,112,128]{2,1,0:T(8,128)(2,1)S(1)} %pad_maximum_fusion.2), channel_id=2, replica_groups=mesh['enc'=2,'blk'=8,'z'=16,'yhi'=2] {'z'}, dimensions={0}, use_global_device_ids=true | all-gather | bytes 974848 | tf_op jit(solution)/shard_map/rows/all_gather | solution.py:266
  159.3 5.5 %head_stats.2 = f32[224,2]{1,0:T(8,128)S(1)} custom-call(s32[5]{0:T(128)S(1)} %stack.42.refs_0_, bf16[8,2,2,112,128]{4,3,2,1,0:T(8,128)(2,1)S(1)} %bitcast.48, f32[1,2048]{1,0:T(1,128)S(1)} %bitcast.56, f32[1,2048]{1,0:T(1,128)S(1)} %bitcast.58, s32[224,1]{1,0:T(8,128)S(1)} %reshape.73.refs_4_, bf16[2048,512]{1,0:T(8,128)(2,1)S(1)} %copy-done, ...), custom_call_target="tpu_custom_call" | custom-call | tf_op jit(solution)/shard_map/head/head_stats/pallas_call | solution.py:174
  164.8 0.2 copy.49
  165.0 1.3 copy-done.1
  166.3 6.4 %head_stats.3 = f32[288,2]{1,0:T(8,128)S(1)} custom-call(s32[5]{0:T(128)S(1)} %stack.42.refs_0_, bf16[8,2,2,144,128]{4,3,2,1,0:T(8,128)(2,1)S(1)} %bitcast.49, f32[1,2048]{1,0:T(1,128)S(1)} %bitcast.57, f32[1,2048]{1,0:T(1,128)S(1)} %bitcast.59, s32[288,1]{1,0:T(8,128)S(1)} %reshape.74.refs_4_, bf16[2048,512]{1,0:T(8,128)(2,1)S(1)} %copy-done, ...), custom_call_target="tpu_custom_call" | custom-call | tf_op jit(solution)/shard_map/head/head_stats/pallas_call | solution.py:174
  172.7 0.2 copy.50
  172.9 0.1 maximum_bitcast_fusion
  172.9 0.1 copy.51
  173.0 28.1 %all_to_all.11 = f32[64,2,16]{2,1,0:T(2,128)S(1)} all-to-all(f32[64,2,16]{2,1,0:T(2,128)S(1)} %bitcast.62), channel_id=1, replica_groups=mesh['enc'=2,'blk'=8,'z'=16,'yhi'=2] {'enc','z','yhi'}, dimensions={0} | all-to-all | bytes 16384 | tf_op jit(solution)/shard_map/merge/all_to_all | solution.py:284
  201.2 0.1 reshape.66
  201.3 0.1 slice_reduce_fusion.1
  201.4 0.1 fusion.1
  201.5 0.6 reshape.67
  (27 shorter events, 0.2 us)
Async XLA Ops:
  6.5 158.5 %all-gather.4.cloned.1.call-start = ((), (), s32[]{:S(2)}) async-start(), calls=%async_computation.2 | async-start | bytes 1253376 | tf_op jit(solution)/shard_map/rows/all_gather | solution.py:266
  8.6 0.9 copy-start.2
  9.5 0.9 copy-start.3
  10.4 0.8 copy-start.4
  11.3 0.8 copy-start.5
  12.1 64.2 %copy-start = (bf16[2048,512]{1,0:T(8,128)(2,1)S(1)}, bf16[2048,512]{1,0:T(8,128)(2,1)}, u32[]{:S(2)}) copy-start(bf16[2048,512]{1,0:T(8,128)(2,1)} %refs_5_.1) | copy-start | bytes 6291460
  76.3 49.1 %collective-permute-start.2 = (bf16[2048,512]{1,0:T(8,128)(2,1)S(1)}, bf16[2048,512]{1,0:T(8,128)(2,1)}, u32[]{:S(2)}, u32[]{:S(2)}) collective-permute-start(bf16[2048,512]{1,0:T(8,128)(2,1)S(1)} %copy-done), channel_id=1, source_target_pairs={{0,1},{1,0},{2,3},{3,2},{4,5},{5,4},{6,7},{7,6},{8,9},{9,8},{10,11... | collective-permute-start | bytes 6291464 | tf_op jit(solution)/shard_map/weights/ppermute | solution.py:226
  82.0 77.4 %copy-start.6 = (f32[2048]{0:T(1024)S(1)}, f32[2048]{0:T(1024)}, u32[]{:S(2)}) copy-start(f32[2048]{0:T(1024)} %param.17) | copy-start | bytes 24580
  82.0 77.4 %copy-start.7 = (f32[2048]{0:T(1024)S(1)}, f32[2048]{0:T(1024)}, u32[]{:S(2)}) copy-start(f32[2048]{0:T(1024)} %param.18) | copy-start | bytes 24580
  84.6 4.0 %collective-permute-start = (bf16[256,128]{1,0:T(8,128)(2,1)S(1)}, bf16[256,128]{1,0:T(8,128)(2,1)S(1)}, u32[]{:S(2)}, u32[]{:S(2)}) collective-permute-start(bf16[256,128]{1,0:T(8,128)(2,1)S(1)} %get-tuple-element.16), channel_id=1, source_target_pairs={{0,256},{256,0},{1,257},{257,1},{2,258},{258,2},{3,259},{259,3},{4... | collective-permute-start | bytes 196616 | tf_op jit(solution)/shard_map/halves/ppermute | solution.py:254
  89.3 70.1 %collective-permute-start.1 = (bf16[2048,512]{1,0:T(8,128)(2,1)S(1)}, bf16[2048,512]{1,0:T(8,128)(2,1)}, u32[]{:S(2)}, u32[]{:S(2)}) collective-permute-start(bf16[2048,512]{1,0:T(8,128)(2,1)S(1)} %copy-done), channel_id=1, source_target_pairs={{0,256},{256,0},{1,257},{257,1},{2,258},{258,2},{3,259},{259,3},{4... | collective-permute-start | bytes 6291464 | tf_op jit(solution)/shard_map/weights/ppermute | solution.py:227
  125.4 34.0 %collective-permute-start.3 = (bf16[2048,512]{1,0:T(8,128)(2,1)}, bf16[2048,512]{1,0:T(8,128)(2,1)}, u32[]{:S(2)}, u32[]{:S(2)}) collective-permute-start(bf16[2048,512]{1,0:T(8,128)(2,1)} %collective-permute-done.2.refs_7_), channel_id=1, source_target_pairs={{0,256},{256,0},{1,257},{257,1},{2,258},{258,2},{3,259},{259,3},{4... | collective-permute-start | bytes 6291464 | tf_op jit(solution)/shard_map/weights/ppermute | solution.py:228
  165.0 1.3 copy-start.1
Sparse Core Ops, SparseCore 0:
  89.4 54.8 all-gather.3

commit v3 on v2

--- a/solution.py
+++ b/solution.py
@@ -20,39 +20,69 @@
 F32 = jnp.float32
 MIB = 1024 * 1024
 
-VOC = ("z", "yhi")
+VOC = ("zh", "zl", "yhi")
 SWAP = [(0, 1), (1, 0)]
+CROSS = [(0, 3), (3, 0), (1, 2), (2, 1)]
 EARLY_SHARE = 14 / 32
 
 
-def pack_kernel(parts, q_ref, r_ref, k_ref, v_ref, out_ref):
-    mem_rows = k_ref.shape[0]
-    piece = q_ref.shape[0] // parts
+def pack_kernel(parts, *refs):
+    sources, out_ref, (q, r, k, v, dec, mem, target), sems = (
+        refs[:7],
+        refs[7],
+        refs[8:15],
+        refs[15],
+    )
+    held = (q, r, k, v, dec, mem, target)
+    copies = [
+        pltpu.make_async_copy(source, buffer, sems.at[index])
+        for index, (source, buffer) in enumerate(zip(sources, held))
+    ]
+    for copy in copies:
+        copy.start()
+    for copy in copies:
+        copy.wait()
+    mem_rows = k.shape[0]
+    rows = q.shape[0]
+    piece = rows // parts
     at_q = 2 * mem_rows
-    for head in range(q_ref.shape[1] // HEAD_DIM):
+    note_rows = out_ref.shape[1] - at_q - 2 * piece
+    wide = lambda a: jnp.pad(a.astype(F32), ((0, 0), (0, HEAD_DIM - a.shape[1])))
+    row = lax.broadcasted_iota(jnp.int32, (note_rows, HEAD_DIM), 0)
+    notes = jnp.zeros((note_rows, HEAD_DIM), F32)
+    for index, value in enumerate((dec[...], mem[...], target[...] // 256, target[...] % 256)):
+        notes = jnp.where(row == index, wide(value), notes)
+    notes = notes.astype(BF16)
+    for head in range(q.shape[1] // HEAD_DIM):
         lanes = pl.ds(head * HEAD_DIM, HEAD_DIM)
         for part in range(parts):
             to = head * parts + part
-            rows = pl.ds(part * piece, piece)
-            out_ref[to, pl.ds(0, mem_rows)] = k_ref[:, lanes]
-            out_ref[to, pl.ds(mem_rows, mem_rows)] = v_ref[:, lanes]
-            out_ref[to, pl.ds(at_q, piece)] = q_ref[rows, lanes]
-            out_ref[to, pl.ds(at_q + piece, piece)] = r_ref[rows, lanes]
-
-
-def pack(q, r, k, v, parts):
+            own = pl.ds(part * piece, piece)
+            out_ref[to, pl.ds(0, mem_rows)] = k[:, lanes]
+            out_ref[to, pl.ds(mem_rows, mem_rows)] = v[:, lanes]
+            out_ref[to, pl.ds(at_q, piece)] = q[own, lanes]
+            out_ref[to, pl.ds(at_q + piece, piece)] = r[own, lanes]
+            out_ref[to, pl.ds(at_q + 2 * piece, note_rows)] = notes
+
+
+def pack(q, r, k, v, dec, mem, target, parts):
     heads = q.shape[1] // HEAD_DIM
-    depth = 2 * k.shape[0] + 2 * (q.shape[0] // parts)
+    depth = 2 * k.shape[0] + 2 * (q.shape[0] // parts) + 8
+    arrays = (q, r, k, v, dec[None], mem[None], target[None])
 
     def kernel(*refs):
         pack_kernel(parts, *refs)
 
     return pl.pallas_call(
         kernel,
+        in_specs=[pl.BlockSpec(memory_space=pltpu.HBM)] * len(arrays),
+        out_specs=pl.BlockSpec(memory_space=pltpu.VMEM),
         out_shape=jax.ShapeDtypeStruct((heads * parts, depth, HEAD_DIM), BF16),
-        compiler_params=pltpu.CompilerParams(vmem_limit_bytes=16 * MIB),
+        scratch_shapes=[pltpu.VMEM(a.shape, a.dtype) for a in arrays]
+        + [pltpu.SemaphoreType.DMA((len(arrays),))],
+        compiler_params=pltpu.CompilerParams(vmem_limit_bytes=64 * MIB),
         name="pack",
-    )(q, r, k, v)
+    )(*arrays)
 
 
 def attend_kernel(piece, q_ref, r_ref, k_ref, v_ref, dec_ref, mem_ref, out_ref):
@@ -100,22 +130,27 @@
 
 
 def head_kernel(vocab, info_ref, x_ref, gain_ref, bias_ref, t_ref, *rest):
-    slabs = len(rest) - 5
+    slabs = len(rest) - 7
     w_refs = rest[:slabs]
-    out_ref, held, normed, logits, sems = rest[slabs:]
+    out_ref, held, x_held, normed, logits, sems, x_sems = rest[slabs:]
+    heads, sets, halves, rows, chunk = x_ref.shape
+    x_copies = [
+        pltpu.make_async_copy(x_ref.at[:, group], x_held.at[:, group], x_sems.at[group])
+        for group in range(sets)
+    ]
     copies = [
         pltpu.make_async_copy(w_refs[k], held.at[k], sems.at[k]) for k in range(slabs)
     ]
-    for copy in copies:
+    for copy in x_copies + copies:
         copy.start()
-    heads, sets, halves, rows, chunk = x_ref.shape
     mine = info_ref[slabs]
     step = 16
     for group in range(sets):
+        x_copies[group].wait()
         for low in range(0, rows, step):
             at = pl.ds(low, step)
             parts = [
-                x_ref[head, group, half, at].astype(F32)
+                x_held[head, group, half, at].astype(F32)
                 for half in range(halves)
                 for head in range(heads)
             ]
@@ -171,17 +206,20 @@
         head_kernel(vocab, *refs)
 
     vmem = pl.BlockSpec(memory_space=pltpu.VMEM)
+    hbm = pl.BlockSpec(memory_space=pltpu.HBM)
     return pl.pallas_call(
         kernel,
-        in_specs=[pl.BlockSpec(memory_space=pltpu.SMEM), vmem, vmem, vmem, vmem]
-        + [pl.BlockSpec(memory_space=pl.ANY)] * len(slabs),
+        in_specs=[pl.BlockSpec(memory_space=pltpu.SMEM), hbm, vmem, vmem, vmem]
+        + [hbm] * len(slabs),
         out_specs=vmem,
         out_shape=jax.ShapeDtypeStruct((total, 2), F32),
         scratch_shapes=[
             pltpu.VMEM((len(slabs), D, width), BF16),
+            pltpu.VMEM(x.shape, BF16),
             pltpu.VMEM((total, D), BF16),
             pltpu.VMEM((total, len(slabs) * width), F32),
             pltpu.SemaphoreType.DMA((len(slabs),)),
+            pltpu.SemaphoreType.DMA((sets,)),
         ],
         compiler_params=pltpu.CompilerParams(vmem_limit_bytes=40 * MIB),
         name="head_stats",
@@ -200,8 +238,10 @@
     ln_bias,
     head_weight,
 ):
-    enc, z, yhi = lax.axis_index("enc"), lax.axis_index("z"), lax.axis_index("yhi")
-    enc_count, z_count, y_count = (lax.axis_size(name) for name in ("enc", "z", "yhi"))
+    enc, zh, zl, yhi = (lax.axis_index(name) for name in ("enc", "zh", "zl", "yhi"))
+    enc_count, y_count = lax.axis_size("enc"), lax.axis_size("yhi")
+    z = zh * lax.axis_size("zl") + zl
+    z_count = lax.axis_size("zh") * lax.axis_size("zl")
     voc_count = z_count * y_count
     heads = queries.shape[1] // HEAD_DIM
     parts = voc_count // heads
@@ -212,30 +252,25 @@
     width = head_weight.shape[1]
     vocab = width * voc_count * enc_count
 
-    with jax.named_scope("pack"):
-        message = pack(queries, residual, mem_keys, mem_values, parts)
-        first = jnp.concatenate([dec_ids, mem_ids, jnp.zeros((128 - rows - mem_rows,), jnp.int32)])
-        second = jnp.concatenate([targets // 256, targets % 256])
-        notes = jnp.stack([first, second]).astype(BF16)
-        notes = jnp.broadcast_to(jnp.pad(notes, ((0, 6), (0, 0)))[None], (voc_count, 8, HEAD_DIM))
-        message = jnp.concatenate([message, notes], axis=1)
-    with jax.named_scope("spread"):
-        got = lax.all_to_all(message, VOC, 0, 0, tiled=True)
-    got, head_weight = lax.optimization_barrier((got, head_weight))
     with jax.named_scope("weights"):
         weight_y = lax.ppermute(head_weight, "yhi", SWAP)
         weight_e = lax.ppermute(head_weight, "enc", SWAP)
-        weight_ye = lax.ppermute(weight_y, "enc", SWAP)
-
+        weight_ye = lax.ppermute(head_weight, ("enc", "yhi"), CROSS)
+    with jax.named_scope("pack"):
+        message = pack(
+            queries, residual, mem_keys, mem_values, dec_ids, mem_ids, targets, parts
+        )
+    with jax.named_scope("spread"):
+        got = lax.all_to_all(message, VOC, 0, 0, tiled=True)
     with jax.named_scope("attention"):
         at_q = 2 * mem_rows
         take = lambda low, count: got[:, low : low + count].reshape(-1, HEAD_DIM)
-        noted = got[:, at_q + 2 * piece : at_q + 2 * piece + 2].astype(jnp.int32)
+        noted = got[:, at_q + 2 * piece : at_q + 2 * piece + 4].astype(jnp.int32)
         dec = lax.dynamic_slice_in_dim(
-            noted[:, 0], ((z % sets) * y_count + yhi) * piece, piece, 1
+            noted[:, 0, :rows], (zl * y_count + yhi) * piece, piece, 1
         ).reshape(-1, 1)
-        mem = noted[:, 0, rows : rows + mem_rows].reshape(1, -1)
-        target = noted[:, 1, :rows] * 256 + noted[:, 1, rows:]
+        mem = noted[:, 1, :mem_rows].reshape(1, -1)
+        target = noted[:, 2, :rows] * 256 + noted[:, 3, :rows]
         target = target.reshape(voc_count, sets, y_count * enc_count, slice_rows)
         target = lax.dynamic_index_in_dim(target, yhi * enc_count + enc, 2, False)
         target = target.transpose(1, 0, 2)
@@ -249,35 +284,51 @@
             piece,
             enc_count,
         )
+    early = int(voc_count * EARLY_SHARE)
+    cut = early * slice_rows
     with jax.named_scope("halves"):
         kept = lax.dynamic_index_in_dim(halves, enc, 0, False)
-        handed = lax.ppermute(
-            lax.dynamic_index_in_dim(halves, 1 - enc, 0, False), "enc", SWAP
-        )
-        shard = jnp.stack([kept, handed])
-    early = int(voc_count * EARLY_SHARE)
-    slab = lambda e, y: ((e * voc_count) + z * y_count + y) * width
-    info = jnp.stack(
-        [slab(enc, yhi), slab(1 - enc, yhi), slab(enc, 1 - yhi), slab(1 - enc, 1 - yhi), enc]
-    ).astype(jnp.int32)
-    found = []
-    for low, high in ((early, voc_count), (0, early)):
-        with jax.named_scope("rows"):
-            full = lax.all_gather(shard[:, low * slice_rows : high * slice_rows], "z", axis=0)
-            full = full.reshape((heads, sets) + full.shape[1:])
+        passed = lax.dynamic_index_in_dim(halves, 1 - enc, 0, False)
+        handed = lax.ppermute(passed, "enc", SWAP)
+        kept_beside = lax.ppermute(kept[cut:], "zl", SWAP)
+        handed_beside = lax.ppermute(passed[cut:], ("enc", "zl"), CROSS)
+        late_shard = jnp.stack(
+            [jnp.stack([kept[cut:], handed[cut:]]), jnp.stack([kept_beside, handed_beside])]
+        )
+        early_shard = jnp.stack([kept[:cut], handed[:cut]])
+    def head(full, target):
         with jax.named_scope("head"):
             stats = head_stats(
                 full,
                 ln_gain[None],
                 ln_bias[None],
-                target[:, low:high].reshape(-1, 1),
+                target.reshape(-1, 1),
                 (head_weight, weight_e, weight_y, weight_ye),
                 info,
                 vocab,
             )
-            found.append(stats.reshape(sets, high - low, slice_rows, 2))
+            return stats.reshape(sets, -1, slice_rows, 2)
+
+    with jax.named_scope("rows"):
+        late_full = lax.all_gather(late_shard, "zh", axis=0)
+        early_full = lax.all_gather(early_shard, ("zh", "zl"), axis=0)
+        early_full = early_full.reshape((heads, sets) + early_full.shape[1:])
+    slab = lambda e, y: ((e * voc_count) + z * y_count + y) * width
+    info = jnp.stack(
+        [
+            slab(enc, yhi),
+            slab(1 - enc, yhi),
+            slab(enc, 1 - yhi),
+            slab(1 - enc, 1 - yhi),
+            enc,
+        ]
+    ).astype(jnp.int32)
+
+    early_stats = head(early_full, target[:, :early])
+    swapped = lambda a: jnp.where(zl == 0, a, a[::-1])
+    late_stats = swapped(head(late_full, swapped(target[:, early:])))
     with jax.named_scope("merge"):
-        stats = jnp.concatenate(found[::-1], axis=1).transpose(1, 3, 0, 2)
+        stats = jnp.concatenate([early_stats, late_stats], axis=1).transpose(1, 3, 0, 2)
         stats = jnp.broadcast_to(
             stats.reshape(1, voc_count, 2, -1), (enc_count, voc_count, 2, sets * slice_rows)
         )
@@ -295,8 +346,8 @@
 def solution(mesh):
     shape = dict(mesh.shape)
     fine = Mesh(
-        mesh.devices.reshape(shape["enc"], shape["blk"], shape["voc"] // 2, 2),
-        ("enc", "blk", "z", "yhi"),
+        mesh.devices.reshape(shape["enc"], shape["blk"], shape["voc"] // 4, 2, 2),
+        ("enc", "blk") + VOC,
     )
     held = ("blk",) + VOC
     in_specs = (

time: 209 us -> 184 us (0.88)
  blocking collectives: 121 us -> 64.9 us
  starting transfers between devices: 15 us -> 38.2 us
  waiting for transfers between devices: 34.7 us -> 46.3 us
  local copies, waits for them, and re-layouts: 7.21 us -> 3.67 us
  other arithmetic: 3.1 us -> 0.97 us
    all_to_all x1 -> x0, blocking collectives: 64 us -> none  [per_device(): got = lax.all_to_all(message, VOC, 0, 0, tiled=True)]
    all_to_all x0 -> x1, waiting for transfers between devices: none -> 35.5 us  [per_device(): got = lax.all_to_all(message, VOC, 0, 0, tiled=True)]
    ppermute x1, waiting for transfers between devices: 33.8 us -> 0.01 us  [per_device(): weight_y = lax.ppermute(head_weight, 'yhi', SWAP)]
    all_to_all x0 -> x1, starting transfers between devices: none -> 18.7 us  [per_device(): got = lax.all_to_all(message, VOC, 0, 0, tiled=True)]
    ppermute x2 -> x4, waiting for transfers between devices: 0.88 us -> 10.8 us  [the longest x1 9.96 us: per_device(): weight_ye = lax.ppermute(head_weight, ('enc', 'yhi'), CROSS)]
    all_gather x1, blocking collectives: 28.6 us -> 35.9 us  [per_device(): early_full = lax.all_gather(early_shard, ('zh', 'zl'), axis=0)]
    ppermute x2 -> x4, starting transfers between devices: 7.7 us -> 11.7 us  [the longest x1 5.49 us: per_device(): handed_beside = lax.ppermute(passed[cut:], ('enc', 'zl'), CROSS)]
    unnamed x16 -> x8, local copies, waits for them, and re-layouts: 4.76 us -> 1.28 us
  transfers between devices with their start and end apart: 5 -> 8, of which waited for: 2 -> 3; matrix products, arithmetic and copies ran while one was open for 1% -> 1% of each run, Pallas kernels for 4% -> 4%
where the time goes in v3:
time: 184 us; the launch traced here: 183 us
  blocking collectives  64.9 us (35%)
  waiting for transfers between devices  46.3 us (25%)
  starting transfers between devices  38.2 us (21%)
  Pallas kernels  15.3 us (8%)
  between operations  13.8 us (8%)
  local copies, waits for them, and re-layouts  3.67 us (2%)
    all_gather x1, blocking collectives, per_device(): early_full = lax.all_gather(early_shard, ('zh', 'zl'), axis=0)  35.9 us
    all_to_all x1, waiting for transfers between devices, per_device(): got = lax.all_to_all(message, VOC, 0, 0, tiled=True)  35.5 us
    all_to_all x1, blocking collectives, per_device(): lax.all_to_all(stats.reshape(enc_count * voc_count, 2, -1), ('enc',) + VO...  29 us
    all_to_all x1, starting transfers between devices, per_device(): got = lax.all_to_all(message, VOC, 0, 0, tiled=True)  18.7 us
    pallas_call x2, Pallas kernels, head_stats(): pl.pallas_call(kernel, in_specs=[pl.BlockSpec(memory_space=pltpu.SMEM), h...  10.7 us
    ppermute x1, waiting for transfers between devices, per_device(): weight_ye = lax.ppermute(head_weight, ('enc', 'yhi'), CROSS)  9.96 us
    ppermute x1, starting transfers between devices, per_device(): handed_beside = lax.ppermute(passed[cut:], ('enc', 'zl'), CROSS)  5.49 us
    ppermute x1, starting transfers between devices, per_device(): weight_y = lax.ppermute(head_weight, 'yhi', SWAP)  4.93 us
  transfers between devices with their start and end apart: 8, of which 3 were waited for; matrix products, arithmetic and copies ran while one was open for 1% of the time, Pallas kernels for 4%

profile of v3, /device:TPU:1, one launch (start us, length us, event | category | flops | bytes accessed | tf_op | source)
XLA Modules:
  0.0 183.1 jit_solution(2643950666804266422)
XLA Ops:
  6.5 2.1 %pack.1 = bf16[32,104,128]{2,1,0:T(8,128)(2,1)} custom-call(bf16[64,1024]{1,0:T(8,128)(2,1)} %refs_0_.1, bf16[64,1024]{1,0:T(8,128)(2,1)} %refs_1_.1, bf16[32,1024]{1,0:T(8,128)(2,1)} %refs_2_.1, bf16[32,1024]{1,0:T(8,128)(2,1)} %refs_3_.1, s32[1,64]{1,0:T(1,128)} %bitcast.78, s32[1,32]{1,0:T(1,128)} %bitcast.79, s32[1,64]{1,0:T(1,128)} %bitcast.80), custom_call_target="tpu_custom_call" | custom-call | tf_op jit(solution)/shard_map/pack/pack/pallas_call | solution.py:76
  8.6 18.7 %all-to-all-start = ((bf16[32,104,128]{2,1,0:T(8,128)(2,1)}), bf16[32,104,128]{2,1,0:T(8,128)(2,1)S(1)}, u32[]{:S(2)}, u32[]{:S(2)}) async-start(bf16[32,104,128]{2,1,0:T(8,128)(2,1)} %pack.1), calls=%async_computation | async-start | bytes 1703936 | tf_op jit(solution)/shard_map/spread/all_to_all | solution.py:264
  27.3 0.0 all-gather.4.cloned.1.call-start
  27.4 2.9 %collective-permute-start.1 = (bf16[2048,512]{1,0:T(8,128)(2,1)}, bf16[2048,512]{1,0:T(8,128)(2,1)}, u32[]{:S(2)}, u32[]{:S(2)}) collective-permute-start(bf16[2048,512]{1,0:T(8,128)(2,1)} %refs_5_.3), channel_id=1, source_target_pairs={{0,256},{256,0},{1,257},{257,1},{2,258},{258,2},{3,259},{259,3},{4... | collective-permute-start | bytes 6291464 | tf_op jit(solution)/shard_map/weights/ppermute | solution.py:257
  30.2 4.9 %collective-permute-start.2 = (bf16[2048,512]{1,0:T(8,128)(2,1)}, bf16[2048,512]{1,0:T(8,128)(2,1)}, u32[]{:S(2)}, u32[]{:S(2)}) collective-permute-start(bf16[2048,512]{1,0:T(8,128)(2,1)} %refs_5_.3), channel_id=1, source_target_pairs={{0,1},{1,0},{2,3},{3,2},{4,5},{5,4},{6,7},{7,6},{8,9},{9,8},{10,11... | collective-permute-start | bytes 6291464 | tf_op jit(solution)/shard_map/weights/ppermute | solution.py:256
  35.2 2.0 %collective-permute-start.3 = (bf16[2048,512]{1,0:T(8,128)(2,1)}, bf16[2048,512]{1,0:T(8,128)(2,1)}, u32[]{:S(2)}, u32[]{:S(2)}) collective-permute-start(bf16[2048,512]{1,0:T(8,128)(2,1)} %refs_5_.3), channel_id=1, source_target_pairs={{0,257},{257,0},{1,256},{256,1},{2,259},{259,2},{3,258},{258,3},{4... | collective-permute-start | bytes 6291464 | tf_op jit(solution)/shard_map/weights/ppermute | solution.py:258
  37.2 35.5 %all-to-all-done = bf16[32,104,128]{2,1,0:T(8,128)(2,1)S(1)} async-done(((bf16[32,104,128]{2,1,0:T(8,128)(2,1)}), bf16[32,104,128]{2,1,0:T(8,128)(2,1)S(1)}, u32[]{:S(2)}, u32[]{:S(2)}) %all-to-all-start) | async-done | bytes 852000 | tf_op jit(solution)/shard_map/spread/all_to_all | solution.py:264
  72.7 0.1 slice_reduce_fusion.2
  72.9 0.1 dynamic-slice_reduce_fusion
  73.0 0.2 reshape.71.refs_4_
  73.2 0.1 squeeze.19.refs_5_
  73.3 0.0 copy-start
  73.3 0.0 copy-start.2
  73.3 0.0 copy-start.3
  73.3 2.5 %attend.1 = bf16[2,256,128]{2,1,0:T(8,128)(2,1)S(1)} custom-call(bf16[512,128]{1,0:T(8,128)(2,1)S(1)} %bitcast.65, bf16[512,128]{1,0:T(8,128)(2,1)S(1)} %bitcast.64, bf16[1024,128]{1,0:T(8,128)(2,1)S(1)} %bitcast.62, bf16[1024,128]{1,0:T(8,128)(2,1)S(1)} %bitcast.61, s32[512,1]{1,0:T(8,128)S(1)} %reshape.71.refs_4_, s32[1,1024]{1,0:T(1,128)S(1)} %squeeze.19.refs_5_), custom_call_target="tpu_custom_call" | custom-call | tf_op jit(solution)/shard_map/attention/attend/pallas_call | solution.py:114
  75.9 1.9 %collective-permute-start.4 = (bf16[144,128]{1,0:T(8,128)(2,1)S(1)}, bf16[144,128]{1,0:T(8,128)(2,1)S(1)}, u32[]{:S(2)}, u32[]{:S(2)}) collective-permute-start(bf16[144,128]{1,0:T(8,128)(2,1)S(1)} %bitcast.72), channel_id=1, source_target_pairs={{0,2},{2,0},{1,3},{3,1},{4,6},{6,4},{5,7},{7,5},{8,10},{10,8},{9,1... | collective-permute-start | bytes 110600 | tf_op jit(solution)/shard_map/halves/ppermute | solution.py:293
  77.8 5.5 %collective-permute-start.5 = (bf16[144,128]{1,0:T(8,128)(2,1)S(1)}, bf16[144,128]{1,0:T(8,128)(2,1)S(1)}, u32[]{:S(2)}, u32[]{:S(2)}) collective-permute-start(bf16[144,128]{1,0:T(8,128)(2,1)S(1)} %get-tuple-element.12), channel_id=1, source_target_pairs={{0,258},{258,0},{2,256},{256,2},{1,259},{259,1},{3,257},{257,3},{4... | collective-permute-start | bytes 110600 | tf_op jit(solution)/shard_map/halves/ppermute | solution.py:294
  83.3 0.0 collective-permute-done.4
  83.4 2.3 %collective-permute-start = (bf16[256,128]{1,0:T(8,128)(2,1)S(1)}, bf16[256,128]{1,0:T(8,128)(2,1)S(1)}, u32[]{:S(2)}, u32[]{:S(2)}) collective-permute-start(bf16[256,128]{1,0:T(8,128)(2,1)S(1)} %dynamic-slice_bitcast_fusion), channel_id=1, source_target_pairs={{0,256},{256,0},{1,257},{257,1},{2,258},{258,2},{3,259},{259,3},{4... | collective-permute-start | bytes 196616 | tf_op jit(solution)/shard_map/halves/ppermute | solution.py:292
  85.6 0.0 collective-permute-done.5
  85.6 0.9 collective-permute-done
  86.5 0.7 pad_maximum_fusion
  87.2 0.0 all-gather.4.cloned.1.call-update
  87.2 0.1 stack.55.refs_0_
  87.3 0.1 copy.47
  87.4 0.1 slice.94
  87.5 0.1 copy.48
  87.6 0.1 reshape.72.refs_4_
  87.7 0.1 copy.50
  87.8 0.1 reshape.73.refs_4_
  87.9 35.9 %all-gather = bf16[32,112,128]{2,1,0:T(8,128)(2,1)S(1)} all-gather(bf16[2,112,128]{2,1,0:T(8,128)(2,1)S(1)} %pad_maximum_fusion.1), channel_id=2, replica_groups=mesh['enc'=2,'blk'=8,'zh'=8,'zl'=2,'yhi'=2] {'zh','zl'}, dimensions={0}, use_global_device_ids=true | all-gather | bytes 974848 | tf_op jit(solution)/shard_map/rows/all_gather | solution.py:314
  123.9 0.0 collective-permute-done.1.refs_6_
  123.9 0.0 collective-permute-done.2.refs_7_
  123.9 10.0 %collective-permute-done.3.refs_8_ = bf16[2048,512]{1,0:T(8,128)(2,1)} collective-permute-done((bf16[2048,512]{1,0:T(8,128)(2,1)}, bf16[2048,512]{1,0:T(8,128)(2,1)}, u32[]{:S(2)}, u32[]{:S(2)}) %collective-permute-start.3) | collective-permute-done | bytes 2097184 | tf_op jit(solution)/shard_map/weights/ppermute | solution.py:258
  133.8 0.0 copy-done
  133.8 0.0 copy-done.2
  133.9 5.0 %head_stats.2 = f32[224,2]{1,0:T(8,128)S(1)} custom-call(s32[5]{0:T(128)S(1)} %stack.55.refs_0_, bf16[8,2,2,112,128]{4,3,2,1,0:T(8,128)(2,1)S(1)} %bitcast.59, f32[1,2048]{1,0:T(1,128)S(1)} %bitcast.67, f32[1,2048]{1,0:T(1,128)S(1)} %bitcast.69, s32[224,1]{1,0:T(8,128)S(1)} %reshape.72.refs_4_, bf16[2048,512]{1,0:T(8,128)(2,1)S(1)} %copy-done, ...), custom_call_target="tpu_custom_call" | custom-call | tf_op jit(solution)/shard_map/head/head_stats/pallas_call | solution.py:210
  138.8 0.2 copy.54
  139.0 1.3 copy-done.1
  140.3 5.7 %head_stats.3 = f32[288,2]{1,0:T(8,128)S(1)} custom-call(s32[5]{0:T(128)S(1)} %stack.55.refs_0_, bf16[8,2,2,144,128]{4,3,2,1,0:T(8,128)(2,1)S(1)} %bitcast.60, f32[1,2048]{1,0:T(1,128)S(1)} %bitcast.68, f32[1,2048]{1,0:T(1,128)S(1)} %bitcast.70, s32[288,1]{1,0:T(8,128)S(1)} %reshape.73.refs_4_, bf16[2048,512]{1,0:T(8,128)(2,1)S(1)} %copy-done, ...), custom_call_target="tpu_custom_call" | custom-call | tf_op jit(solution)/shard_map/head/head_stats/pallas_call | solution.py:210
  146.0 0.2 copy.53
  146.2 0.1 maximum_bitcast_fusion.2
  146.3 0.1 copy.55
  146.4 29.0 %all_to_all.10 = f32[64,2,16]{2,1,0:T(2,128)S(1)} all-to-all(f32[64,2,16]{2,1,0:T(2,128)S(1)} %bitcast.71), channel_id=1, replica_groups=mesh['enc'=2,'blk'=8,'zh'=8,'zl'=2,'yhi'=2] {'enc','zh','zl','yhi'}, dimensions={0} | all-to-all | bytes 16384 | tf_op jit(solution)/shard_map/merge/all_to_all | solution.py:335
  175.4 0.1 reshape.66
  175.5 0.1 slice_reduce_fusion.1
  175.6 0.1 fusion.1
  175.7 0.6 reshape.67
  (23 shorter events, 0.3 us)
Async XLA Ops:
  8.6 64.1 %all-to-all-start = ((bf16[32,104,128]{2,1,0:T(8,128)(2,1)}), bf16[32,104,128]{2,1,0:T(8,128)(2,1)S(1)}, u32[]{:S(2)}, u32[]{:S(2)}) async-start(bf16[32,104,128]{2,1,0:T(8,128)(2,1)} %pack.1), calls=%async_computation | async-start | bytes 1703936 | tf_op jit(solution)/shard_map/spread/all_to_all | solution.py:264
  27.3 111.7 %all-gather.4.cloned.1.call-start = ((), (), s32[]{:S(2)}) async-start(), calls=%async_computation.2 | async-start | bytes 1327104 | tf_op jit(solution)/shard_map/rows/all_gather | solution.py:313
  27.4 96.5 %collective-permute-start.1 = (bf16[2048,512]{1,0:T(8,128)(2,1)}, bf16[2048,512]{1,0:T(8,128)(2,1)}, u32[]{:S(2)}, u32[]{:S(2)}) collective-permute-start(bf16[2048,512]{1,0:T(8,128)(2,1)} %refs_5_.3), channel_id=1, source_target_pairs={{0,256},{256,0},{1,257},{257,1},{2,258},{258,2},{3,259},{259,3},{4... | collective-permute-start | bytes 6291464 | tf_op jit(solution)/shard_map/weights/ppermute | solution.py:257
  30.2 93.6 %collective-permute-start.2 = (bf16[2048,512]{1,0:T(8,128)(2,1)}, bf16[2048,512]{1,0:T(8,128)(2,1)}, u32[]{:S(2)}, u32[]{:S(2)}) collective-permute-start(bf16[2048,512]{1,0:T(8,128)(2,1)} %refs_5_.3), channel_id=1, source_target_pairs={{0,1},{1,0},{2,3},{3,2},{4,5},{5,4},{6,7},{7,6},{8,9},{9,8},{10,11... | collective-permute-start | bytes 6291464 | tf_op jit(solution)/shard_map/weights/ppermute | solution.py:256
  35.2 98.7 %collective-permute-start.3 = (bf16[2048,512]{1,0:T(8,128)(2,1)}, bf16[2048,512]{1,0:T(8,128)(2,1)}, u32[]{:S(2)}, u32[]{:S(2)}) collective-permute-start(bf16[2048,512]{1,0:T(8,128)(2,1)} %refs_5_.3), channel_id=1, source_target_pairs={{0,257},{257,0},{1,256},{256,1},{2,259},{259,2},{3,258},{258,3},{4... | collective-permute-start | bytes 6291464 | tf_op jit(solution)/shard_map/weights/ppermute | solution.py:258
  73.3 60.5 %copy-start = (bf16[2048,512]{1,0:T(8,128)(2,1)S(1)}, bf16[2048,512]{1,0:T(8,128)(2,1)}, u32[]{:S(2)}) copy-start(bf16[2048,512]{1,0:T(8,128)(2,1)} %refs_5_.3) | copy-start | bytes 6291460
  73.3 60.5 %copy-start.2 = (f32[2048]{0:T(1024)S(1)}, f32[2048]{0:T(1024)}, u32[]{:S(2)}) copy-start(f32[2048]{0:T(1024)} %param.17) | copy-start | bytes 24580
  73.3 60.5 %copy-start.3 = (f32[2048]{0:T(1024)S(1)}, f32[2048]{0:T(1024)}, u32[]{:S(2)}) copy-start(f32[2048]{0:T(1024)} %param.18) | copy-start | bytes 24580
  75.9 7.5 %collective-permute-start.4 = (bf16[144,128]{1,0:T(8,128)(2,1)S(1)}, bf16[144,128]{1,0:T(8,128)(2,1)S(1)}, u32[]{:S(2)}, u32[]{:S(2)}) collective-permute-start(bf16[144,128]{1,0:T(8,128)(2,1)S(1)} %bitcast.72), channel_id=1, source_target_pairs={{0,2},{2,0},{1,3},{3,1},{4,6},{6,4},{5,7},{7,5},{8,10},{10,8},{9,1... | collective-permute-start | bytes 110600 | tf_op jit(solution)/shard_map/halves/ppermute | solution.py:293
  77.8 7.8 %collective-permute-start.5 = (bf16[144,128]{1,0:T(8,128)(2,1)S(1)}, bf16[144,128]{1,0:T(8,128)(2,1)S(1)}, u32[]{:S(2)}, u32[]{:S(2)}) collective-permute-start(bf16[144,128]{1,0:T(8,128)(2,1)S(1)} %get-tuple-element.12), channel_id=1, source_target_pairs={{0,258},{258,0},{2,256},{256,2},{1,259},{259,1},{3,257},{257,3},{4... | collective-permute-start | bytes 110600 | tf_op jit(solution)/shard_map/halves/ppermute | solution.py:294
  83.4 3.1 %collective-permute-start = (bf16[256,128]{1,0:T(8,128)(2,1)S(1)}, bf16[256,128]{1,0:T(8,128)(2,1)S(1)}, u32[]{:S(2)}, u32[]{:S(2)}) collective-permute-start(bf16[256,128]{1,0:T(8,128)(2,1)S(1)} %dynamic-slice_bitcast_fusion), channel_id=1, source_target_pairs={{0,256},{256,0},{1,257},{257,1},{2,258},{258,2},{3,259},{259,3},{4... | collective-permute-start | bytes 196616 | tf_op jit(solution)/shard_map/halves/ppermute | solution.py:292
  139.0 1.3 copy-start.1
Sparse Core Ops, SparseCore 0:
  87.3 44.7 all-gather.3

commit v4 on v3

--- a/solution.py
+++ b/solution.py
@@ -20,10 +20,9 @@
 F32 = jnp.float32
 MIB = 1024 * 1024
 
-VOC = ("zh", "zl", "yhi")
+Z = ("zq", "zr")
+VOC = Z + ("yhi",)
 SWAP = [(0, 1), (1, 0)]
-CROSS = [(0, 3), (3, 0), (1, 2), (2, 1)]
-EARLY_SHARE = 14 / 32
 
 
 def pack_kernel(parts, *refs):
@@ -129,101 +128,125 @@
     )(q, r, k, v, dec, mem)
 
 
-def head_kernel(vocab, info_ref, x_ref, gain_ref, bias_ref, t_ref, *rest):
-    slabs = len(rest) - 7
-    w_refs = rest[:slabs]
-    out_ref, held, x_held, normed, logits, sems, x_sems = rest[slabs:]
-    heads, sets, halves, rows, chunk = x_ref.shape
-    x_copies = [
-        pltpu.make_async_copy(x_ref.at[:, group], x_held.at[:, group], x_sems.at[group])
-        for group in range(sets)
-    ]
+def head_kernel(vocab, slabs, places, sets, info_ref, gain_ref, bias_ref, t_ref, *rest):
+    out_ref, held, normed, logits, columns, turned, sems = rest[-7:]
+    x_refs, w_refs = rest[: -7 - slabs], rest[-7 - slabs : -7]
+    turns = 1 + max(place[2] for place in places)
     copies = [
         pltpu.make_async_copy(w_refs[k], held.at[k], sems.at[k]) for k in range(slabs)
     ]
-    for copy in x_copies + copies:
+    for copy in copies:
         copy.start()
-    mine = info_ref[slabs]
+    enc, z, own_rows = (info_ref[slabs + index] for index in range(3))
+    halves, rows, chunk = x_refs[0].shape[1:]
+    heads = len(places) // sets
+    total = sets * rows
+    width = held.shape[2]
+    side = columns.shape[1]
     step = 16
+    lane = lax.broadcasted_iota(jnp.int32, (step, side), 1)
+
+    voc_count = t_ref.shape[0]
+    share = rows // voc_count
+    filler = jnp.zeros((side - voc_count, side), F32)
+    turned[...] = jnp.transpose(jnp.concatenate([t_ref[...], filler], axis=0))
+    orders = [lax.rem(z + group, sets) for group in range(sets)]
     for group in range(sets):
-        x_copies[group].wait()
+        at = pl.multiple_of(orders[group] * (side // 2 // sets) + own_rows, share)
+        block = turned[pl.ds(at, share)]
+        for voc in range(voc_count):
+            columns[pl.ds(group * rows + voc * share, share)] = jnp.broadcast_to(
+                block[:, voc : voc + 1], (share, side)
+            )
+
+    for group in range(sets):
+        order = [
+            (place, half)
+            for place in places
+            if place[2] % sets == group
+            for half in range(halves)
+        ]
+        bases = []
+        for (_, _, turn, index), half in order:
+            head = index * (turns // sets) + lax.rem(z + turn, turns) // sets
+            at_half = jnp.where(enc == 0, half, 1 - half)
+            bases.append(pl.multiple_of((at_half * heads + head) * chunk, chunk))
         for low in range(0, rows, step):
             at = pl.ds(low, step)
             parts = [
-                x_held[head, group, half, at].astype(F32)
-                for half in range(halves)
-                for head in range(heads)
+                x_refs[place[0]][place[1], half, at].astype(F32) for place, half in order
             ]
             mean = jnp.sum(sum(parts[1:], parts[0]), axis=1, keepdims=True) * (1.0 / D)
             parts = [part - mean for part in parts]
             squares = [part * part for part in parts]
             var = jnp.sum(sum(squares[1:], squares[0]), axis=1, keepdims=True) * (1.0 / D)
             scale = lax.rsqrt(var + LN_EPS)
-            for half in range(halves):
-                base = jnp.where(mine == 0, half, 1 - half) * (heads * chunk)
-                for head in range(heads):
-                    lanes = pl.ds(pl.multiple_of(base + head * chunk, chunk), chunk)
-                    value = parts[half * heads + head] * scale * gain_ref[:, lanes]
-                    normed[pl.ds(group * rows + low, step), lanes] = (
-                        value + bias_ref[:, lanes]
-                    ).astype(BF16)
-    total = sets * rows
-    width = held.shape[2]
+            for base, part in zip(bases, parts):
+                lanes = pl.ds(base, chunk)
+                value = part * scale * gain_ref[:, lanes] + bias_ref[:, lanes]
+                normed[pl.ds(group * rows + low, step), lanes] = value.astype(BF16)
+
     for k in range(slabs):
         copies[k].wait()
         logits[:, pl.ds(k * width, width)] = jnp.dot(
             normed[...], held[k], preferred_element_type=F32
         )
-    lane = lax.broadcasted_iota(jnp.int32, (step, 128), 1)
+
     for low in range(0, total, step):
         at = pl.ds(low, step)
-        target = t_ref[at]
-        top = logits[at, pl.ds(0, 128)]
-        for col in range(128, slabs * width, 128):
-            top = jnp.maximum(top, logits[at, pl.ds(col, 128)])
+        target = columns[at].astype(jnp.int32)
+        top = logits[at, pl.ds(0, side)]
+        for col in range(side, slabs * width, side):
+            top = jnp.maximum(top, logits[at, pl.ds(col, side)])
         top = jnp.max(top, axis=1, keepdims=True)
-        exps = sums = picks = jnp.zeros((step, 128), F32)
+        exps = sums = picks = jnp.zeros((step, side), F32)
         for k in range(slabs):
-            offset = target - info_ref[k]
-            for col in range(0, width, 128):
-                part = logits[at, pl.ds(k * width + col, 128)]
+            offset = target - info_ref[k] - lane
+            for col in range(0, width, side):
+                part = logits[at, pl.ds(k * width + col, side)]
                 exps = exps + jnp.exp(part - top)
                 sums = sums + part
-                picks = picks + jnp.where(lane == offset - col, part, 0.0)
+                picks = picks + jnp.where(offset == col, part, 0.0)
         lse = top + jnp.log(jnp.sum(exps, axis=1, keepdims=True))
         line = (1.0 - EPS_SMOOTH) * picks + (EPS_SMOOTH / vocab) * sums
         line = jnp.sum(line, axis=1, keepdims=True)
-        pair = lax.broadcasted_iota(jnp.int32, (step, 2), 1)
-        out_ref[at] = jnp.where(pair == 0, lse, line)
-
-
-def head_stats(x, gain, bias, targets, slabs, info, vocab):
-    heads, sets, halves, rows, chunk = x.shape
-    total = sets * rows
+        columns[at] = jnp.where(lane == 0, lse, line)
+
+    for group in range(sets):
+        for low in range(0, rows, side):
+            block = jnp.transpose(columns[pl.ds(group * rows + low, side)])
+            lanes = pl.ds(pl.multiple_of(orders[group] * rows + low, side), side)
+            out_ref[:, lanes] = block[: out_ref.shape[0]]
+
+
+def head_stats(xs, places, sets, gain, bias, targets, slabs, info, vocab):
+    total = sets * xs[0].shape[2]
     width = slabs[0].shape[1]
 
     def kernel(*refs):
-        head_kernel(vocab, *refs)
+        head_kernel(vocab, len(slabs), places, sets, *refs)
 
     vmem = pl.BlockSpec(memory_space=pltpu.VMEM)
     hbm = pl.BlockSpec(memory_space=pltpu.HBM)
-    return pl.pallas_call(
+    stats = pl.pallas_call(
         kernel,
-        in_specs=[pl.BlockSpec(memory_space=pltpu.SMEM), hbm, vmem, vmem, vmem]
+        in_specs=[pl.BlockSpec(memory_space=pltpu.SMEM), vmem, vmem, vmem]
+        + [vmem] * len(xs)
         + [hbm] * len(slabs),
         out_specs=vmem,
-        out_shape=jax.ShapeDtypeStruct((total, 2), F32),
+        out_shape=jax.ShapeDtypeStruct((8, total), F32),
         scratch_shapes=[
             pltpu.VMEM((len(slabs), D, width), BF16),
-            pltpu.VMEM(x.shape, BF16),
             pltpu.VMEM((total, D), BF16),
             pltpu.VMEM((total, len(slabs) * width), F32),
+            pltpu.VMEM((total, 128), F32),
+            pltpu.VMEM((128, 128), F32),
             pltpu.SemaphoreType.DMA((len(slabs),)),
-            pltpu.SemaphoreType.DMA((sets,)),
         ],
         compiler_params=pltpu.CompilerParams(vmem_limit_bytes=40 * MIB),
         name="head_stats",
-    )(info, x, gain, bias, targets, *slabs)
+    )(info, gain, bias, targets, *xs, *slabs)
+    return stats[:2]
 
 
 def per_device(
@@ -238,10 +261,8 @@
     ln_bias,
     head_weight,
 ):
-    enc, zh, zl, yhi = (lax.axis_index(name) for name in ("enc", "zh", "zl", "yhi"))
-    enc_count, y_count = lax.axis_size("enc"), lax.axis_size("yhi")
-    z = zh * lax.axis_size("zl") + zl
-    z_count = lax.axis_size("zh") * lax.axis_size("zl")
+    enc, z, yhi = (lax.axis_index(name) for name in ("enc", Z, "yhi"))
+    enc_count, z_count, y_count = (lax.axis_size(name) for name in ("enc", Z, "yhi"))
     voc_count = z_count * y_count
     heads = queries.shape[1] // HEAD_DIM
     parts = voc_count // heads
@@ -255,25 +276,22 @@
     with jax.named_scope("weights"):
         weight_y = lax.ppermute(head_weight, "yhi", SWAP)
         weight_e = lax.ppermute(head_weight, "enc", SWAP)
-        weight_ye = lax.ppermute(head_weight, ("enc", "yhi"), CROSS)
     with jax.named_scope("pack"):
         message = pack(
             queries, residual, mem_keys, mem_values, dec_ids, mem_ids, targets, parts
         )
     with jax.named_scope("spread"):
         got = lax.all_to_all(message, VOC, 0, 0, tiled=True)
+        got, weight_e = lax.optimization_barrier((got, weight_e))
     with jax.named_scope("attention"):
         at_q = 2 * mem_rows
         take = lambda low, count: got[:, low : low + count].reshape(-1, HEAD_DIM)
         noted = got[:, at_q + 2 * piece : at_q + 2 * piece + 4].astype(jnp.int32)
         dec = lax.dynamic_slice_in_dim(
-            noted[:, 0, :rows], (zl * y_count + yhi) * piece, piece, 1
+            noted[:, 0, :rows], (z % sets * y_count + yhi) * piece, piece, 1
         ).reshape(-1, 1)
         mem = noted[:, 1, :mem_rows].reshape(1, -1)
-        target = noted[:, 2, :rows] * 256 + noted[:, 3, :rows]
-        target = target.reshape(voc_count, sets, y_count * enc_count, slice_rows)
-        target = lax.dynamic_index_in_dim(target, yhi * enc_count + enc, 2, False)
-        target = target.transpose(1, 0, 2)
+        target = (noted[:, 2] * 256 + noted[:, 3]).astype(F32)
         halves = attend(
             take(at_q, piece),
             take(at_q + piece, piece),
@@ -284,51 +302,59 @@
             piece,
             enc_count,
         )
-    early = int(voc_count * EARLY_SHARE)
-    cut = early * slice_rows
     with jax.named_scope("halves"):
         kept = lax.dynamic_index_in_dim(halves, enc, 0, False)
         passed = lax.dynamic_index_in_dim(halves, 1 - enc, 0, False)
-        handed = lax.ppermute(passed, "enc", SWAP)
-        kept_beside = lax.ppermute(kept[cut:], "zl", SWAP)
-        handed_beside = lax.ppermute(passed[cut:], ("enc", "zl"), CROSS)
-        late_shard = jnp.stack(
-            [jnp.stack([kept[cut:], handed[cut:]]), jnp.stack([kept_beside, handed_beside])]
-        )
-        early_shard = jnp.stack([kept[:cut], handed[:cut]])
-    def head(full, target):
-        with jax.named_scope("head"):
-            stats = head_stats(
-                full,
-                ln_gain[None],
-                ln_bias[None],
-                target.reshape(-1, 1),
-                (head_weight, weight_e, weight_y, weight_ye),
-                info,
-                vocab,
+        shard = jnp.stack([kept, lax.ppermute(passed, "enc", SWAP)])
+    with jax.named_scope("rows"):
+        up = [(i, (i + 1) % z_count) for i in range(z_count)]
+        down = [(i, (i - 1) % z_count) for i in range(z_count)]
+        fours = lax.all_gather(shard, "zq", axis=0)
+        fours, weight_y = lax.optimization_barrier((fours, weight_y))
+        below, above = lax.ppermute(fours, Z, up), lax.ppermute(fours, Z, down)
+        cut = fours.shape[0] // 2
+        opposite = lax.ppermute(below[:cut], Z, up), lax.ppermute(above[cut:], Z, down)
+        bundles = [fours, above, opposite[0], opposite[1], below]
+        places = [
+            (ref, index - first, turn, index)
+            for turn, ref, first, last in (
+                (0, 0, 0, 2 * cut),
+                (1, 1, 0, 2 * cut),
+                (2, 2, 0, cut),
+                (2, 3, cut, 2 * cut),
+                (3, 4, 0, 2 * cut),
             )
-            return stats.reshape(sets, -1, slice_rows, 2)
-
-    with jax.named_scope("rows"):
-        late_full = lax.all_gather(late_shard, "zh", axis=0)
-        early_full = lax.all_gather(early_shard, ("zh", "zl"), axis=0)
-        early_full = early_full.reshape((heads, sets) + early_full.shape[1:])
-    slab = lambda e, y: ((e * voc_count) + z * y_count + y) * width
-    info = jnp.stack(
-        [
-            slab(enc, yhi),
-            slab(1 - enc, yhi),
-            slab(enc, 1 - yhi),
-            slab(1 - enc, 1 - yhi),
-            enc,
+            for index in range(first, last)
         ]
-    ).astype(jnp.int32)
-
-    early_stats = head(early_full, target[:, :early])
-    swapped = lambda a: jnp.where(zl == 0, a, a[::-1])
-    late_stats = swapped(head(late_full, swapped(target[:, early:])))
+    with jax.named_scope("weights"):
+        weight_ye = lax.ppermute(weight_y, "enc", SWAP)
+    with jax.named_scope("head"):
+        slab = lambda e, y: ((e * voc_count) + z * y_count + y) * width
+        info = jnp.stack(
+            [
+                slab(enc, yhi),
+                slab(1 - enc, yhi),
+                slab(enc, 1 - yhi),
+                slab(1 - enc, 1 - yhi),
+                enc,
+                z,
+                yhi * piece + enc * slice_rows,
+            ]
+        ).astype(jnp.int32)
+        stats = head_stats(
+            bundles,
+            places,
+            sets,
+            ln_gain[None],
+            ln_bias[None],
+            target,
+            (head_weight, weight_e, weight_y, weight_ye),
+            info,
+            vocab,
+        )
+        stats = stats.reshape(2, sets, voc_count, slice_rows)
     with jax.named_scope("merge"):
-        stats = jnp.concatenate([early_stats, late_stats], axis=1).transpose(1, 3, 0, 2)
+        stats = stats.transpose(2, 0, 1, 3)
         stats = jnp.broadcast_to(
             stats.reshape(1, voc_count, 2, -1), (enc_count, voc_count, 2, sets * slice_rows)
         )
@@ -346,7 +372,7 @@
 def solution(mesh):
     shape = dict(mesh.shape)
     fine = Mesh(
-        mesh.devices.reshape(shape["enc"], shape["blk"], shape["voc"] // 4, 2, 2),
+        mesh.devices.reshape(shape["enc"], shape["blk"], shape["voc"] // 8, 4, 2),
         ("enc", "blk") + VOC,
     )
     held = ("blk",) + VOC

time: 184 us -> 175 us (0.951)
  between operations: 13.8 us -> 0.34 us
  blocking collectives: 64.9 us -> 54.1 us
  starting transfers between devices: 38.2 us -> 46.2 us
  waiting for transfers between devices: 46.3 us -> 53.3 us
  local copies, waits for them, and re-layouts: 3.67 us -> 6.5 us
    all_gather x1, blocking collectives: 35.9 us -> 24.9 us  [per_device(): fours = lax.all_gather(shard, 'zq', axis=0)]
    ppermute x4 -> x6, starting transfers between devices: 11.7 us -> 19.7 us  [the longest x2 6.49 us: per_device(): below, above = (lax.ppermute(fours, Z, up), lax.ppermute(fours, Z, down))]
    ppermute x4 -> x6, waiting for transfers between devices: 10.8 us -> 15.7 us  [the longest x2 10.1 us: per_device(): below, above = (lax.ppermute(fours, Z, up), lax.ppermute(fours, Z, down))]
    unnamed x8 -> x14, local copies, waits for them, and re-layouts: 1.28 us -> 3.45 us
    all_to_all x1, waiting for transfers between devices: 35.5 us -> 37.6 us  [per_device(): got = lax.all_to_all(message, VOC, 0, 0, tiled=True)]
    pallas_call x2 -> x1, Pallas kernels: 10.7 us -> 9.36 us  [head_stats(): pl.pallas_call(kernel, in_specs=[pl.BlockSpec(memory_space=pltpu.SMEM), v...]
  transfers between devices with their start and end apart: 8 -> 9, of which waited for: 3 -> 5; matrix products, arithmetic and copies ran while one was open for 1% -> 1% of each run, Pallas kernels for 4% -> 1%
where the time goes in v4:
time: 175 us
  blocking collectives  54.1 us (31%)
  waiting for transfers between devices  53.3 us (30%)
  starting transfers between devices  46.2 us (26%)
  Pallas kernels  14 us (8%)
  local copies, waits for them, and re-layouts  6.5 us (4%)
    all_to_all x1, waiting for transfers between devices, per_device(): got = lax.all_to_all(message, VOC, 0, 0, tiled=True)  37.6 us
    all_to_all x1, blocking collectives, per_device(): lax.all_to_all(stats.reshape(enc_count * voc_count, 2, -1), ('enc',) + VO...  29.1 us
    all_gather x1, blocking collectives, per_device(): fours = lax.all_gather(shard, 'zq', axis=0)  24.9 us
    all_to_all x1, starting transfers between devices, per_device(): got = lax.all_to_all(message, VOC, 0, 0, tiled=True)  18.7 us
    ppermute x2, waiting for transfers between devices, per_device(): below, above = (lax.ppermute(fours, Z, up), lax.ppermute(fours, Z, down))  10.1 us
    pallas_call x1, Pallas kernels, head_stats(): pl.pallas_call(kernel, in_specs=[pl.BlockSpec(memory_space=pltpu.SMEM), v...  9.36 us
    ppermute x2, starting transfers between devices, per_device(): below, above = (lax.ppermute(fours, Z, up), lax.ppermute(fours, Z, down))  6.49 us
    ppermute x1, starting transfers between devices, per_device(): weight_y = lax.ppermute(head_weight, 'yhi', SWAP)  4.93 us
  transfers between devices with their start and end apart: 9, of which 5 were waited for; matrix products, arithmetic and copies ran while one was open for 1% of the time, Pallas kernels for 1%

profile of v4, /device:TPU:1, one launch (start us, length us, event | category | flops | bytes accessed | tf_op | source)
XLA Modules:
  0.0 174.5 jit_solution(3711184707954986894)
XLA Ops:
  0.0 2.1 %pack.1 = bf16[32,104,128]{2,1,0:T(8,128)(2,1)} custom-call(bf16[64,1024]{1,0:T(8,128)(2,1)} %refs_0_.1, bf16[64,1024]{1,0:T(8,128)(2,1)} %refs_1_.1, bf16[32,1024]{1,0:T(8,128)(2,1)} %refs_2_.1, bf16[32,1024]{1,0:T(8,128)(2,1)} %refs_3_.1, s32[1,64]{1,0:T(1,128)} %bitcast.56, s32[1,32]{1,0:T(1,128)} %bitcast.57, s32[1,64]{1,0:T(1,128)} %bitcast.58), custom_call_target="tpu_custom_call" | custom-call | tf_op jit(solution)/shard_map/pack/pack/pallas_call | solution.py:75
  2.1 18.7 %all-to-all-start = ((bf16[32,104,128]{2,1,0:T(8,128)(2,1)}), bf16[32,104,128]{2,1,0:T(8,128)(2,1)S(1)}, u32[]{:S(2)}, u32[]{:S(2)}) async-start(bf16[32,104,128]{2,1,0:T(8,128)(2,1)} %pack.1), calls=%async_computation | async-start | bytes 1703936 | tf_op jit(solution)/shard_map/spread/all_to_all | solution.py:284
  20.8 2.9 %collective-permute-start = (bf16[2048,512]{1,0:T(8,128)(2,1)}, bf16[2048,512]{1,0:T(8,128)(2,1)S(1)}, u32[]{:S(2)}, u32[]{:S(2)}) collective-permute-start(bf16[2048,512]{1,0:T(8,128)(2,1)} %refs_9_.1), channel_id=1, source_target_pairs={{0,256},{256,0},{1,257},{257,1},{2,258},{258,2},{3,259},{259,3},{4... | collective-permute-start | bytes 6291464 | tf_op jit(solution)/shard_map/weights/ppermute | solution.py:278
  23.7 4.9 %collective-permute-start.2 = (bf16[2048,512]{1,0:T(8,128)(2,1)}, bf16[2048,512]{1,0:T(8,128)(2,1)}, u32[]{:S(2)}, u32[]{:S(2)}) collective-permute-start(bf16[2048,512]{1,0:T(8,128)(2,1)} %refs_9_.1), channel_id=1, source_target_pairs={{0,1},{1,0},{2,3},{3,2},{4,5},{5,4},{6,7},{7,6},{8,9},{9,8},{10,11... | collective-permute-start | bytes 6291464 | tf_op jit(solution)/shard_map/weights/ppermute | solution.py:277
  28.6 0.0 collective-permute-done.refs_10_
  28.6 0.0 copy-start.1
  28.6 37.6 %all-to-all-done = bf16[32,104,128]{2,1,0:T(8,128)(2,1)S(1)} async-done(((bf16[32,104,128]{2,1,0:T(8,128)(2,1)}), bf16[32,104,128]{2,1,0:T(8,128)(2,1)S(1)}, u32[]{:S(2)}, u32[]{:S(2)}) %all-to-all-start) | async-done | bytes 852000 | tf_op jit(solution)/shard_map/spread/all_to_all | solution.py:284
  66.2 0.1 copy.22
  66.4 0.1 squeeze.15.refs_5_
  66.5 0.1 constant_dynamic-slice_fusion.1
  66.5 0.2 reshape.46.refs_4_
  66.7 0.0 copy-done.1
  66.7 0.0 copy-start
  66.7 0.0 copy-start.5
  66.8 0.0 copy-start.6
  66.8 2.6 %attend.1 = bf16[2,256,128]{2,1,0:T(8,128)(2,1)S(1)} custom-call(bf16[512,128]{1,0:T(8,128)(2,1)S(1)} %bitcast.49, bf16[512,128]{1,0:T(8,128)(2,1)S(1)} %bitcast.48, bf16[1024,128]{1,0:T(8,128)(2,1)S(1)} %bitcast.47, bf16[1024,128]{1,0:T(8,128)(2,1)S(1)} %bitcast.46, s32[512,1]{1,0:T(8,128)S(1)} %reshape.46.refs_4_, s32[1,1024]{1,0:T(1,128)S(1)} %squeeze.15.refs_5_), custom_call_target="tpu_custom_call" | custom-call | tf_op jit(solution)/shard_map/attention/attend/pallas_call | solution.py:113
  69.4 3.9 %collective-permute-start.1 = (bf16[256,128]{1,0:T(8,128)(2,1)S(1)}, bf16[256,128]{1,0:T(8,128)(2,1)S(1)}, u32[]{:S(2)}, u32[]{:S(2)}) collective-permute-start(bf16[256,128]{1,0:T(8,128)(2,1)S(1)} %get-tuple-element.20), channel_id=1, source_target_pairs={{0,256},{256,0},{1,257},{257,1},{2,258},{258,2},{3,259},{259,3},{4... | collective-permute-start | bytes 196616 | tf_op jit(solution)/shard_map/halves/ppermute | solution.py:308
  73.3 0.9 collective-permute-done.1
  74.2 24.9 %all-gather = bf16[8,256,128]{2,1,0:T(8,128)(2,1)S(1)} all-gather(bf16[2,256,128]{2,1,0:T(8,128)(2,1)S(1)} %pad_maximum_fusion), channel_id=2, replica_groups=mesh['enc'=2,'blk'=8,'zq'=4,'zr'=4,'yhi'=2] {'zq'}, dimensions={0}, use_global_device_ids=true | all-gather | bytes 655360 | tf_op jit(solution)/shard_map/rows/all_gather | solution.py:312
  99.1 0.0 collective-permute-done.2.refs_11_
  99.1 2.9 %collective-permute-start.7 = (bf16[2048,512]{1,0:T(8,128)(2,1)}, bf16[2048,512]{1,0:T(8,128)(2,1)}, u32[]{:S(2)}, u32[]{:S(2)}) collective-permute-start(bf16[2048,512]{1,0:T(8,128)(2,1)} %collective-permute-done.2.refs_11_), channel_id=1, source_target_pairs={{0,256},{256,0},{1,257},{257,1},{2,258},{258,2},{3,259},{259,3},{4... | collective-permute-start | bytes 6291464 | tf_op jit(solution)/shard_map/weights/ppermute | solution.py:330
  102.0 1.9 %collective-permute-start.4 = (bf16[4,2,256,128]{3,2,1,0:T(8,128)(2,1)S(1)}, bf16[4,2,256,128]{3,2,1,0:T(8,128)(2,1)S(1)}, u32[]{:S(2)}, u32[]{:S(2)}) collective-permute-start(bf16[4,2,256,128]{3,2,1,0:T(8,128)(2,1)S(1)} %bitcast.43), channel_id=1, source_target_pairs={{0,2},{2,4},{4,6},{6,8},{8,10},{10,12},{12,14},{14,16},{16,18},{18... | collective-permute-start | bytes 1572872 | tf_op jit(solution)/shard_map/rows/ppermute | solution.py:314
  103.9 4.6 %collective-permute-start.3 = (bf16[4,2,256,128]{3,2,1,0:T(8,128)(2,1)S(1)}, bf16[4,2,256,128]{3,2,1,0:T(8,128)(2,1)S(1)}, u32[]{:S(2)}, u32[]{:S(2)}) collective-permute-start(bf16[4,2,256,128]{3,2,1,0:T(8,128)(2,1)S(1)} %bitcast.44), channel_id=1, source_target_pairs={{0,30},{2,0},{4,2},{6,4},{8,6},{10,8},{12,10},{14,12},{16,14},{18,... | collective-permute-start | bytes 1572872 | tf_op jit(solution)/shard_map/rows/ppermute | solution.py:314
  108.5 10.1 %collective-permute-done.4.refs_8_ = bf16[4,2,256,128]{3,2,1,0:T(8,128)(2,1)S(1)} collective-permute-done((bf16[4,2,256,128]{3,2,1,0:T(8,128)(2,1)S(1)}, bf16[4,2,256,128]{3,2,1,0:T(8,128)(2,1)S(1)}, u32[]{:S(2)}, u32[]{:S(2)}) %collective-permute-start.4) | collective-permute-done | bytes 524320 | tf_op jit(solution)/shard_map/rows/ppermute | solution.py:314
  118.6 0.7 slice.61
  119.3 1.9 %collective-permute-start.5 = (bf16[2,2,256,128]{3,2,1,0:T(8,128)(2,1)}, bf16[2,2,256,128]{3,2,1,0:T(8,128)(2,1)S(1)}, u32[]{:S(2)}, u32[]{:S(2)}) collective-permute-start(bf16[2,2,256,128]{3,2,1,0:T(8,128)(2,1)} %slice.61), channel_id=1, source_target_pairs={{0,2},{2,4},{4,6},{6,8},{8,10},{10,12},{12,14},{14,16},{16,18},{18... | collective-permute-start | bytes 786440 | tf_op jit(solution)/shard_map/rows/ppermute | solution.py:316
  121.3 0.0 collective-permute-done.3.refs_5_
  121.3 0.7 slice.62
  122.0 0.8 copy-done.3
  122.8 4.6 %collective-permute-start.6 = (bf16[2,2,256,128]{3,2,1,0:T(8,128)(2,1)}, bf16[2,2,256,128]{3,2,1,0:T(8,128)(2,1)}, u32[]{:S(2)}, u32[]{:S(2)}) collective-permute-start(bf16[2,2,256,128]{3,2,1,0:T(8,128)(2,1)} %slice.62), channel_id=1, source_target_pairs={{0,30},{2,0},{4,2},{6,4},{8,6},{10,8},{12,10},{14,12},{16,14},{18,... | collective-permute-start | bytes 786440 | tf_op jit(solution)/shard_map/rows/ppermute | solution.py:316
  127.4 0.1 stack.38.refs_0_
  127.5 2.2 %collective-permute-done.5.refs_6_ = bf16[2,2,256,128]{3,2,1,0:T(8,128)(2,1)S(1)} collective-permute-done((bf16[2,2,256,128]{3,2,1,0:T(8,128)(2,1)}, bf16[2,2,256,128]{3,2,1,0:T(8,128)(2,1)S(1)}, u32[]{:S(2)}, u32[]{:S(2)}) %collective-permute-start.5) | collective-permute-done | bytes 262176 | tf_op jit(solution)/shard_map/rows/ppermute | solution.py:316
  129.7 2.5 %collective-permute-done.6.refs_7_ = bf16[2,2,256,128]{3,2,1,0:T(8,128)(2,1)} collective-permute-done((bf16[2,2,256,128]{3,2,1,0:T(8,128)(2,1)}, bf16[2,2,256,128]{3,2,1,0:T(8,128)(2,1)}, u32[]{:S(2)}, u32[]{:S(2)}) %collective-permute-start.6) | collective-permute-done | bytes 262176 | tf_op jit(solution)/shard_map/rows/ppermute | solution.py:316
  132.2 0.0 collective-permute-done.7.refs_12_
  132.2 0.0 copy-done
  132.2 0.0 copy-done.5
  132.2 0.0 copy-start.2
  132.2 1.6 copy-done.2
  133.8 1.0 copy-done.4
  134.8 9.4 %head_stats.1 = f32[8,512]{1,0:T(8,128)S(1)} custom-call(s32[7]{0:T(128)S(1)} %stack.38.refs_0_, f32[1,2048]{1,0:T(1,128)S(1)} %bitcast.50, f32[1,2048]{1,0:T(1,128)S(1)} %bitcast.51, f32[32,128]{1,0:T(8,128)S(1)} %fusion.3.refs_3_, bf16[4,2,256,128]{3,2,1,0:T(8,128)(2,1)S(1)} %bitcast.45, bf16[4,2,256,128]{3,2,1,0:T(8,128)(2,1)S(1)} %copy-done.4, ...), custom_call_target="tpu_custom_call" | custom-call | tf_op jit(solution)/shard_map/head/head_stats/pallas_call | solution.py:231
  144.2 0.1 reshape.41
  144.3 0.1 copy.24
  144.4 0.1 copy.25
  144.5 29.1 %all_to_all.10 = f32[64,2,16]{2,1,0:T(2,128)S(1)} all-to-all(f32[64,2,16]{2,1,0:T(2,128)S(1)} %bitcast.53), channel_id=1, replica_groups=mesh['enc'=2,'blk'=8,'zq'=4,'zr'=4,'yhi'=2] {'enc','zq','zr','yhi'}, dimensions={0} | all-to-all | bytes 16384 | tf_op jit(solution)/shard_map/merge/all_to_all | solution.py:361
  173.6 0.1 reshape.43
  173.8 0.1 slice_reduce_fusion.1
  173.8 0.1 fusion.1
  173.9 0.6 reshape.44
  (16 shorter events, 0.2 us)
Async XLA Ops:
  2.1 64.1 %all-to-all-start = ((bf16[32,104,128]{2,1,0:T(8,128)(2,1)}), bf16[32,104,128]{2,1,0:T(8,128)(2,1)S(1)}, u32[]{:S(2)}, u32[]{:S(2)}) async-start(bf16[32,104,128]{2,1,0:T(8,128)(2,1)} %pack.1), calls=%async_computation | async-start | bytes 1703936 | tf_op jit(solution)/shard_map/spread/all_to_all | solution.py:284
  20.8 7.8 %collective-permute-start = (bf16[2048,512]{1,0:T(8,128)(2,1)}, bf16[2048,512]{1,0:T(8,128)(2,1)S(1)}, u32[]{:S(2)}, u32[]{:S(2)}) collective-permute-start(bf16[2048,512]{1,0:T(8,128)(2,1)} %refs_9_.1), channel_id=1, source_target_pairs={{0,256},{256,0},{1,257},{257,1},{2,258},{258,2},{3,259},{259,3},{4... | collective-permute-start | bytes 6291464 | tf_op jit(solution)/shard_map/weights/ppermute | solution.py:278
  23.7 75.4 %collective-permute-start.2 = (bf16[2048,512]{1,0:T(8,128)(2,1)}, bf16[2048,512]{1,0:T(8,128)(2,1)}, u32[]{:S(2)}, u32[]{:S(2)}) collective-permute-start(bf16[2048,512]{1,0:T(8,128)(2,1)} %refs_9_.1), channel_id=1, source_target_pairs={{0,1},{1,0},{2,3},{3,2},{4,5},{5,4},{6,7},{7,6},{8,9},{9,8},{10,11... | collective-permute-start | bytes 6291464 | tf_op jit(solution)/shard_map/weights/ppermute | solution.py:277
  28.6 38.1 %copy-start.1 = (bf16[2048,512]{1,0:T(8,128)(2,1)}, bf16[2048,512]{1,0:T(8,128)(2,1)S(1)}, u32[]{:S(2)}) copy-start(bf16[2048,512]{1,0:T(8,128)(2,1)S(1)} %collective-permute-done.refs_10_) | copy-start | bytes 6291460
  66.7 65.4 %copy-start = (bf16[2048,512]{1,0:T(8,128)(2,1)S(1)}, bf16[2048,512]{1,0:T(8,128)(2,1)}, u32[]{:S(2)}) copy-start(bf16[2048,512]{1,0:T(8,128)(2,1)} %refs_9_.1) | copy-start | bytes 6291460
  66.7 65.4 %copy-start.5 = (f32[2048]{0:T(1024)S(1)}, f32[2048]{0:T(1024)}, u32[]{:S(2)}) copy-start(f32[2048]{0:T(1024)} %param.17) | copy-start | bytes 24580
  66.8 65.4 %copy-start.6 = (f32[2048]{0:T(1024)S(1)}, f32[2048]{0:T(1024)}, u32[]{:S(2)}) copy-start(f32[2048]{0:T(1024)} %param.18) | copy-start | bytes 24580
  69.4 4.8 %collective-permute-start.1 = (bf16[256,128]{1,0:T(8,128)(2,1)S(1)}, bf16[256,128]{1,0:T(8,128)(2,1)S(1)}, u32[]{:S(2)}, u32[]{:S(2)}) collective-permute-start(bf16[256,128]{1,0:T(8,128)(2,1)S(1)} %get-tuple-element.20), channel_id=1, source_target_pairs={{0,256},{256,0},{1,257},{257,1},{2,258},{258,2},{3,259},{259,3},{4... | collective-permute-start | bytes 196616 | tf_op jit(solution)/shard_map/halves/ppermute | solution.py:308
  99.1 33.1 %collective-permute-start.7 = (bf16[2048,512]{1,0:T(8,128)(2,1)}, bf16[2048,512]{1,0:T(8,128)(2,1)}, u32[]{:S(2)}, u32[]{:S(2)}) collective-permute-start(bf16[2048,512]{1,0:T(8,128)(2,1)} %collective-permute-done.2.refs_11_), channel_id=1, source_target_pairs={{0,256},{256,0},{1,257},{257,1},{2,258},{258,2},{3,259},{259,3},{4... | collective-permute-start | bytes 6291464 | tf_op jit(solution)/shard_map/weights/ppermute | solution.py:330
  102.0 16.6 %collective-permute-start.4 = (bf16[4,2,256,128]{3,2,1,0:T(8,128)(2,1)S(1)}, bf16[4,2,256,128]{3,2,1,0:T(8,128)(2,1)S(1)}, u32[]{:S(2)}, u32[]{:S(2)}) collective-permute-start(bf16[4,2,256,128]{3,2,1,0:T(8,128)(2,1)S(1)} %bitcast.43), channel_id=1, source_target_pairs={{0,2},{2,4},{4,6},{6,8},{8,10},{10,12},{12,14},{14,16},{16,18},{18... | collective-permute-start | bytes 1572872 | tf_op jit(solution)/shard_map/rows/ppermute | solution.py:314
  103.9 17.4 %collective-permute-start.3 = (bf16[4,2,256,128]{3,2,1,0:T(8,128)(2,1)S(1)}, bf16[4,2,256,128]{3,2,1,0:T(8,128)(2,1)S(1)}, u32[]{:S(2)}, u32[]{:S(2)}) collective-permute-start(bf16[4,2,256,128]{3,2,1,0:T(8,128)(2,1)S(1)} %bitcast.44), channel_id=1, source_target_pairs={{0,30},{2,0},{4,2},{6,4},{8,6},{10,8},{12,10},{14,12},{16,14},{18,... | collective-permute-start | bytes 1572872 | tf_op jit(solution)/shard_map/rows/ppermute | solution.py:314
  119.3 10.3 %collective-permute-start.5 = (bf16[2,2,256,128]{3,2,1,0:T(8,128)(2,1)}, bf16[2,2,256,128]{3,2,1,0:T(8,128)(2,1)S(1)}, u32[]{:S(2)}, u32[]{:S(2)}) collective-permute-start(bf16[2,2,256,128]{3,2,1,0:T(8,128)(2,1)} %slice.61), channel_id=1, source_target_pairs={{0,2},{2,4},{4,6},{6,8},{8,10},{10,12},{12,14},{14,16},{16,18},{18... | collective-permute-start | bytes 786440 | tf_op jit(solution)/shard_map/rows/ppermute | solution.py:316
  122.0 0.8 copy-start.3
  122.8 9.4 %collective-permute-start.6 = (bf16[2,2,256,128]{3,2,1,0:T(8,128)(2,1)}, bf16[2,2,256,128]{3,2,1,0:T(8,128)(2,1)}, u32[]{:S(2)}, u32[]{:S(2)}) collective-permute-start(bf16[2,2,256,128]{3,2,1,0:T(8,128)(2,1)} %slice.62), channel_id=1, source_target_pairs={{0,30},{2,0},{4,2},{6,4},{8,6},{10,8},{12,10},{14,12},{16,14},{18,... | collective-permute-start | bytes 786440 | tf_op jit(solution)/shard_map/rows/ppermute | solution.py:316
  132.2 1.6 copy-start.2
  133.8 1.0 copy-start.4

commit v5 on v4

--- a/solution.py
+++ b/solution.py
@@ -128,20 +128,21 @@
     )(q, r, k, v, dec, mem)
 
 
-def head_kernel(vocab, slabs, places, sets, info_ref, gain_ref, bias_ref, t_ref, *rest):
+def head_kernel(
+    vocab, slabs, places, group, sets, info_ref, gain_ref, bias_ref, t_ref, *rest
+):
     out_ref, held, normed, logits, columns, turned, sems = rest[-7:]
     x_refs, w_refs = rest[: -7 - slabs], rest[-7 - slabs : -7]
-    turns = 1 + max(place[2] for place in places)
     copies = [
         pltpu.make_async_copy(w_refs[k], held.at[k], sems.at[k]) for k in range(slabs)
     ]
     for copy in copies:
         copy.start()
+    turns = 4
     enc, z, own_rows = (info_ref[slabs + index] for index in range(3))
     halves, rows, chunk = x_refs[0].shape[1:]
-    heads = len(places) // sets
-    total = sets * rows
-    width = held.shape[2]
+    heads = len(places)
+    width = w_refs[0].shape[1]
     side = columns.shape[1]
     step = 16
     lane = lax.broadcasted_iota(jnp.int32, (step, side), 1)
@@ -150,41 +151,31 @@
     share = rows // voc_count
     filler = jnp.zeros((side - voc_count, side), F32)
     turned[...] = jnp.transpose(jnp.concatenate([t_ref[...], filler], axis=0))
-    orders = [lax.rem(z + group, sets) for group in range(sets)]
-    for group in range(sets):
-        at = pl.multiple_of(orders[group] * (side // 2 // sets) + own_rows, share)
-        block = turned[pl.ds(at, share)]
-        for voc in range(voc_count):
-            columns[pl.ds(group * rows + voc * share, share)] = jnp.broadcast_to(
-                block[:, voc : voc + 1], (share, side)
-            )
-
-    for group in range(sets):
-        order = [
-            (place, half)
-            for place in places
-            if place[2] % sets == group
-            for half in range(halves)
-        ]
-        bases = []
-        for (_, _, turn, index), half in order:
-            head = index * (turns // sets) + lax.rem(z + turn, turns) // sets
-            at_half = jnp.where(enc == 0, half, 1 - half)
-            bases.append(pl.multiple_of((at_half * heads + head) * chunk, chunk))
-        for low in range(0, rows, step):
-            at = pl.ds(low, step)
-            parts = [
-                x_refs[place[0]][place[1], half, at].astype(F32) for place, half in order
-            ]
-            mean = jnp.sum(sum(parts[1:], parts[0]), axis=1, keepdims=True) * (1.0 / D)
-            parts = [part - mean for part in parts]
-            squares = [part * part for part in parts]
-            var = jnp.sum(sum(squares[1:], squares[0]), axis=1, keepdims=True) * (1.0 / D)
-            scale = lax.rsqrt(var + LN_EPS)
-            for base, part in zip(bases, parts):
-                lanes = pl.ds(base, chunk)
-                value = part * scale * gain_ref[:, lanes] + bias_ref[:, lanes]
-                normed[pl.ds(group * rows + low, step), lanes] = value.astype(BF16)
+    at = pl.multiple_of(lax.rem(z + group, sets) * (side // 2 // sets) + own_rows, share)
+    block = turned[pl.ds(at, share)]
+    for voc in range(voc_count):
+        columns[pl.ds(voc * share, share)] = jnp.broadcast_to(
+            block[:, voc : voc + 1], (share, side)
+        )
+
+    order = [(place, half) for place in places for half in range(halves)]
+    bases = []
+    for (_, _, turn, index), half in order:
+        head = index * (turns // sets) + lax.rem(z + turn, turns) // sets
+        at_half = jnp.where(enc == 0, half, 1 - half)
+        bases.append(pl.multiple_of((at_half * heads + head) * chunk, chunk))
+    for low in range(0, rows, step):
+        at = pl.ds(low, step)
+        parts = [x_refs[place[0]][place[1], half, at].astype(F32) for place, half in order]
+        mean = jnp.sum(sum(parts[1:], parts[0]), axis=1, keepdims=True) * (1.0 / D)
+        parts = [part - mean for part in parts]
+        squares = [part * part for part in parts]
+        var = jnp.sum(sum(squares[1:], squares[0]), axis=1, keepdims=True) * (1.0 / D)
+        scale = lax.rsqrt(var + LN_EPS)
+        for base, part in zip(bases, parts):
+            lanes = pl.ds(base, chunk)
+            value = part * scale * gain_ref[:, lanes] + bias_ref[:, lanes]
+            normed[at, lanes] = value.astype(BF16)
 
     for k in range(slabs):
         copies[k].wait()
@@ -192,7 +183,7 @@
             normed[...], held[k], preferred_element_type=F32
         )
 
-    for low in range(0, total, step):
+    for low in range(0, rows, step):
         at = pl.ds(low, step)
         target = columns[at].astype(jnp.int32)
         top = logits[at, pl.ds(0, side)]
@@ -212,38 +203,41 @@
         line = jnp.sum(line, axis=1, keepdims=True)
         columns[at] = jnp.where(lane == 0, lse, line)
 
-    for group in range(sets):
-        for low in range(0, rows, side):
-            block = jnp.transpose(columns[pl.ds(group * rows + low, side)])
-            lanes = pl.ds(pl.multiple_of(orders[group] * rows + low, side), side)
-            out_ref[:, lanes] = block[: out_ref.shape[0]]
-
-
-def head_stats(xs, places, sets, gain, bias, targets, slabs, info, vocab):
-    total = sets * xs[0].shape[2]
+    for low in range(0, rows, side):
+        block = jnp.transpose(columns[pl.ds(low, side)])
+        out_ref[:, pl.ds(low, side)] = block[: out_ref.shape[0]]
+
+
+def head_stats(xs, places, group, sets, gain, bias, targets, slabs, info, vocab):
+    rows = xs[0].shape[2]
     width = slabs[0].shape[1]
 
     def kernel(*refs):
-        head_kernel(vocab, len(slabs), places, sets, *refs)
+        head_kernel(vocab, len(slabs), places, group, sets, *refs)
 
     vmem = pl.BlockSpec(memory_space=pltpu.VMEM)
     hbm = pl.BlockSpec(memory_space=pltpu.HBM)
     stats = pl.pallas_call(
         kernel,
-        in_specs=[pl.BlockSpec(memory_space=pltpu.SMEM), vmem, vmem, vmem]
-        + [vmem] * len(xs)
+        in_specs=[pl.BlockSpec(memory_space=pltpu.SMEM)]
+        + [vmem] * (3 + len(xs))
         + [hbm] * len(slabs),
         out_specs=vmem,
-        out_shape=jax.ShapeDtypeStruct((8, total), F32),
+        out_shape=jax.ShapeDtypeStruct((8, rows), F32),
         scratch_shapes=[
             pltpu.VMEM((len(slabs), D, width), BF16),
-            pltpu.VMEM((total, D), BF16),
-            pltpu.VMEM((total, len(slabs) * width), F32),
-            pltpu.VMEM((total, 128), F32),
+            pltpu.VMEM((rows, D), BF16),
+            pltpu.VMEM((rows, len(slabs) * width), F32),
+            pltpu.VMEM((rows, 128), F32),
             pltpu.VMEM((128, 128), F32),
             pltpu.SemaphoreType.DMA((len(slabs),)),
         ],
-        compiler_params=pltpu.CompilerParams(vmem_limit_bytes=40 * MIB),
+        compiler_params=pltpu.CompilerParams(vmem_limit_bytes=32 * MIB),
+        cost_estimate=pl.CostEstimate(
+            flops=2 * rows * D * len(slabs) * width,
+            bytes_accessed=2 * D * len(slabs) * width,
+            transcendentals=rows * len(slabs) * width,
+        ),
         name="head_stats",
     )(info, gain, bias, targets, *xs, *slabs)
     return stats[:2]
@@ -311,21 +305,11 @@
         down = [(i, (i - 1) % z_count) for i in range(z_count)]
         fours = lax.all_gather(shard, "zq", axis=0)
         fours, weight_y = lax.optimization_barrier((fours, weight_y))
-        below, above = lax.ppermute(fours, Z, up), lax.ppermute(fours, Z, down)
         cut = fours.shape[0] // 2
-        opposite = lax.ppermute(below[:cut], Z, up), lax.ppermute(above[cut:], Z, down)
-        bundles = [fours, above, opposite[0], opposite[1], below]
-        places = [
-            (ref, index - first, turn, index)
-            for turn, ref, first, last in (
-                (0, 0, 0, 2 * cut),
-                (1, 1, 0, 2 * cut),
-                (2, 2, 0, cut),
-                (2, 3, cut, 2 * cut),
-                (3, 4, 0, 2 * cut),
-            )
-            for index in range(first, last)
-        ]
+        low, high = fours[:cut], fours[cut:]
+        below_low, above_high = lax.ppermute(low, Z, up), lax.ppermute(high, Z, down)
+        below_high, above_low = lax.ppermute(high, Z, up), lax.ppermute(low, Z, down)
+        far_low, far_high = lax.ppermute(below_low, Z, up), lax.ppermute(above_high, Z, down)
     with jax.named_scope("weights"):
         weight_ye = lax.ppermute(weight_y, "enc", SWAP)
     with jax.named_scope("head"):
@@ -341,18 +325,42 @@
                 yhi * piece + enc * slice_rows,
             ]
         ).astype(jnp.int32)
-        stats = head_stats(
-            bundles,
-            places,
-            sets,
-            ln_gain[None],
-            ln_bias[None],
-            target,
-            (head_weight, weight_e, weight_y, weight_ye),
-            info,
-            vocab,
-        )
-        stats = stats.reshape(2, sets, voc_count, slice_rows)
+        halved = lambda ref, turn, first: [
+            (ref, index, turn, first + index) for index in range(cut)
+        ]
+
+        def head(group, xs, places):
+            found = head_stats(
+                xs,
+                places,
+                group,
+                sets,
+                ln_gain[None],
+                ln_bias[None],
+                target,
+                (head_weight, weight_e, weight_y, weight_ye),
+                info,
+                vocab,
+            )
+            return found.reshape(2, 1, voc_count, slice_rows)
+
+        other = head(
+            1,
+            [above_low, above_high, below_low, below_high],
+            halved(0, 1, 0) + halved(1, 1, cut) + halved(2, 3, 0) + halved(3, 3, cut),
+        )
+        same = head(
+            0,
+            [fours, far_low, far_high],
+            [(0, index, 0, index) for index in range(2 * cut)]
+            + halved(1, 2, 0)
+            + halved(2, 2, cut),
+        )
+        stats = jnp.where(
+            z % sets == 0,
+            jnp.concatenate([same, other], axis=1),
+            jnp.concatenate([other, same], axis=1),
+        )
     with jax.named_scope("merge"):
         stats = stats.transpose(2, 0, 1, 3)
         stats = jnp.broadcast_to(

time: 175 us -> 168 us (0.960)
  waiting for transfers between devices: 53.3 us -> 39.3 us
  starting transfers between devices: 46.2 us -> 51.6 us
  Pallas kernels: 14 us -> 16.3 us
    ppermute x4 -> x6, waiting for transfers between devices: 14.8 us -> 0.83 us  [the longest x1 0.82 us: per_device(): lax.ppermute(high, Z, up)]
    ppermute x4 -> x6, starting transfers between devices: 13 us -> 18.2 us  [the longest x1 4.57 us: per_device(): lax.ppermute(above_high, Z, down)]
    pallas_call x1 -> x2, Pallas kernels: 9.36 us -> 11.6 us  [head_stats(): pl.pallas_call(kernel, in_specs=[pl.BlockSpec(memory_space=pltpu.SMEM)] +...]
  transfers between devices with their start and end apart: 9 -> 11, of which waited for: 5 -> 3; matrix products, arithmetic and copies ran while one was open for 1% -> 1% of each run, Pallas kernels for 1% -> 5%
where the time goes in v5:
time: 168 us; the launch traced here: 167 us
  blocking collectives  53.6 us (32%)
  starting transfers between devices  51.6 us (31%)
  waiting for transfers between devices  39.3 us (23%)
  Pallas kernels  16.3 us (10%)
  local copies, waits for them, and re-layouts  5.8 us (3%)
    all_to_all x1, waiting for transfers between devices, per_device(): got = lax.all_to_all(message, VOC, 0, 0, tiled=True)  37.6 us
    all_to_all x1, blocking collectives, per_device(): lax.all_to_all(stats.reshape(enc_count * voc_count, 2, -1), ('enc',) + VO...  28.9 us
    all_gather x1, blocking collectives, per_device(): fours = lax.all_gather(shard, 'zq', axis=0)  24.7 us
    all_to_all x1, starting transfers between devices, per_device(): got = lax.all_to_all(message, VOC, 0, 0, tiled=True)  18.7 us
    pallas_call x2, Pallas kernels, head_stats(): pl.pallas_call(kernel, in_specs=[pl.BlockSpec(memory_space=pltpu.SMEM)] +...  11.6 us
    ppermute x1, starting transfers between devices, per_device(): weight_y = lax.ppermute(head_weight, 'yhi', SWAP)  4.93 us
    ppermute x1, starting transfers between devices, per_device(): lax.ppermute(above_high, Z, down)  4.57 us
    ppermute x1, starting transfers between devices, per_device(): lax.ppermute(high, Z, down)  4.57 us
  transfers between devices with their start and end apart: 11, of which 3 were waited for; matrix products, arithmetic and copies ran while one was open for 1% of the time, Pallas kernels for 5%

profile of v5, /device:TPU:1, one launch (start us, length us, event | category | flops | bytes accessed | tf_op | source)
XLA Modules:
  0.0 167.1 jit_solution(18179254444855749063)
XLA Ops:
  0.0 2.1 %pack.1 = bf16[32,104,128]{2,1,0:T(8,128)(2,1)} custom-call(bf16[64,1024]{1,0:T(8,128)(2,1)} %refs_0_.1, bf16[64,1024]{1,0:T(8,128)(2,1)} %refs_1_.1, bf16[32,1024]{1,0:T(8,128)(2,1)} %refs_2_.1, bf16[32,1024]{1,0:T(8,128)(2,1)} %refs_3_.1, s32[1,64]{1,0:T(1,128)} %bitcast.57, s32[1,32]{1,0:T(1,128)} %bitcast.58, s32[1,64]{1,0:T(1,128)} %bitcast.59), custom_call_target="tpu_custom_call" | custom-call | tf_op jit(solution)/shard_map/pack/pack/pallas_call | solution.py:75
  2.1 18.7 %all-to-all-start = ((bf16[32,104,128]{2,1,0:T(8,128)(2,1)}), bf16[32,104,128]{2,1,0:T(8,128)(2,1)S(1)}, u32[]{:S(2)}, u32[]{:S(2)}) async-start(bf16[32,104,128]{2,1,0:T(8,128)(2,1)} %pack.1), calls=%async_computation | async-start | bytes 1703936 | tf_op jit(solution)/shard_map/spread/all_to_all | solution.py:278
  20.8 2.9 %collective-permute-start = (bf16[2048,512]{1,0:T(8,128)(2,1)}, bf16[2048,512]{1,0:T(8,128)(2,1)S(1)}, u32[]{:S(2)}, u32[]{:S(2)}) collective-permute-start(bf16[2048,512]{1,0:T(8,128)(2,1)} %refs_8_.1), channel_id=1, source_target_pairs={{0,256},{256,0},{1,257},{257,1},{2,258},{258,2},{3,259},{259,3},{4... | collective-permute-start | bytes 6291464 | tf_op jit(solution)/shard_map/weights/ppermute | solution.py:272
  23.7 4.9 %collective-permute-start.2 = (bf16[2048,512]{1,0:T(8,128)(2,1)}, bf16[2048,512]{1,0:T(8,128)(2,1)}, u32[]{:S(2)}, u32[]{:S(2)}) collective-permute-start(bf16[2048,512]{1,0:T(8,128)(2,1)} %refs_8_.1), channel_id=1, source_target_pairs={{0,1},{1,0},{2,3},{3,2},{4,5},{5,4},{6,7},{7,6},{8,9},{9,8},{10,11... | collective-permute-start | bytes 6291464 | tf_op jit(solution)/shard_map/weights/ppermute | solution.py:271
  28.6 0.0 collective-permute-done.refs_8_.refs_9_
  28.6 37.6 %all-to-all-done = bf16[32,104,128]{2,1,0:T(8,128)(2,1)S(1)} async-done(((bf16[32,104,128]{2,1,0:T(8,128)(2,1)}), bf16[32,104,128]{2,1,0:T(8,128)(2,1)S(1)}, u32[]{:S(2)}, u32[]{:S(2)}) %all-to-all-start) | async-done | bytes 852000 | tf_op jit(solution)/shard_map/spread/all_to_all | solution.py:278
  66.2 0.1 copy.22
  66.4 0.1 constant_dynamic-slice_fusion.1
  66.5 0.2 reshape.50.refs_4_
  66.6 0.1 squeeze.15.refs_5_
  66.7 0.0 copy-start
  66.7 0.0 copy-start.4
  66.8 0.0 copy-start.5
  66.8 2.5 %attend.1 = bf16[2,256,128]{2,1,0:T(8,128)(2,1)S(1)} custom-call(bf16[512,128]{1,0:T(8,128)(2,1)S(1)} %bitcast.50, bf16[512,128]{1,0:T(8,128)(2,1)S(1)} %bitcast.49, bf16[1024,128]{1,0:T(8,128)(2,1)S(1)} %bitcast.48, bf16[1024,128]{1,0:T(8,128)(2,1)S(1)} %bitcast.47, s32[512,1]{1,0:T(8,128)S(1)} %reshape.50.refs_4_, s32[1,1024]{1,0:T(1,128)S(1)} %squeeze.15.refs_5_), custom_call_target="tpu_custom_call" | custom-call | tf_op jit(solution)/shard_map/attention/attend/pallas_call | solution.py:113
  69.4 3.9 %collective-permute-start.1 = (bf16[256,128]{1,0:T(8,128)(2,1)S(1)}, bf16[256,128]{1,0:T(8,128)(2,1)S(1)}, u32[]{:S(2)}, u32[]{:S(2)}) collective-permute-start(bf16[256,128]{1,0:T(8,128)(2,1)S(1)} %get-tuple-element.22), channel_id=1, source_target_pairs={{0,256},{256,0},{1,257},{257,1},{2,258},{258,2},{3,259},{259,3},{4... | collective-permute-start | bytes 196616 | tf_op jit(solution)/shard_map/halves/ppermute | solution.py:302
  73.2 0.9 collective-permute-done.1
  74.1 24.7 %all-gather = bf16[8,256,128]{2,1,0:T(8,128)(2,1)S(1)} all-gather(bf16[2,256,128]{2,1,0:T(8,128)(2,1)S(1)} %pad_maximum_fusion), channel_id=2, replica_groups=mesh['enc'=2,'blk'=8,'zq'=4,'zr'=4,'yhi'=2] {'zq'}, dimensions={0}, use_global_device_ids=true | all-gather | bytes 655360 | tf_op jit(solution)/shard_map/rows/all_gather | solution.py:306
  98.8 0.0 collective-permute-done.2.refs_9_.refs_10_
  98.8 3.0 %collective-permute-start.7 = (bf16[2048,512]{1,0:T(8,128)(2,1)}, bf16[2048,512]{1,0:T(8,128)(2,1)}, u32[]{:S(2)}, u32[]{:S(2)}) collective-permute-start(bf16[2048,512]{1,0:T(8,128)(2,1)} %collective-permute-done.2.refs_9_.refs_10_), channel_id=1, source_target_pairs={{0,256},{256,0},{1,257},{257,1},{2,258},{258,2},{3,259},{259,3},{4... | collective-permute-start | bytes 6291464 | tf_op jit(solution)/shard_map/weights/ppermute | solution.py:314
  101.9 0.8 fusion.8
  102.7 1.9 %collective-permute-start.3 = (bf16[2,2,256,128]{3,2,1,0:T(8,128)(2,1)}, bf16[2,2,256,128]{3,2,1,0:T(8,128)(2,1)S(1)}, u32[]{:S(2)}, u32[]{:S(2)}) collective-permute-start(bf16[2,2,256,128]{3,2,1,0:T(8,128)(2,1)} %get-tuple-element.20), channel_id=1, source_target_pairs={{0,2},{2,4},{4,6},{6,8},{8,10},{10,12},{12,14},{14,16},{16,18},{18... | collective-permute-start | bytes 786440 | tf_op jit(solution)/shard_map/rows/ppermute | solution.py:310
  104.6 4.6 %collective-permute-start.5 = (bf16[2,2,256,128]{3,2,1,0:T(8,128)(2,1)}, bf16[2,2,256,128]{3,2,1,0:T(8,128)(2,1)S(1)}, u32[]{:S(2)}, u32[]{:S(2)}) collective-permute-start(bf16[2,2,256,128]{3,2,1,0:T(8,128)(2,1)} %get-tuple-element.19), channel_id=1, source_target_pairs={{0,30},{2,0},{4,2},{6,4},{8,6},{10,8},{12,10},{14,12},{16,14},{18,... | collective-permute-start | bytes 786440 | tf_op jit(solution)/shard_map/rows/ppermute | solution.py:310
  109.2 2.4 %collective-permute-start.8 = (bf16[2,2,256,128]{3,2,1,0:T(8,128)(2,1)}, bf16[2,2,256,128]{3,2,1,0:T(8,128)(2,1)S(1)}, u32[]{:S(2)}, u32[]{:S(2)}) collective-permute-start(bf16[2,2,256,128]{3,2,1,0:T(8,128)(2,1)} %get-tuple-element.20), channel_id=1, source_target_pairs={{0,30},{2,0},{4,2},{6,4},{8,6},{10,8},{12,10},{14,12},{16,14},{18,... | collective-permute-start | bytes 786440 | tf_op jit(solution)/shard_map/rows/ppermute | solution.py:311
  111.6 2.9 %collective-permute-start.9 = (bf16[2,2,256,128]{3,2,1,0:T(8,128)(2,1)}, bf16[2,2,256,128]{3,2,1,0:T(8,128)(2,1)}, u32[]{:S(2)}, u32[]{:S(2)}) collective-permute-start(bf16[2,2,256,128]{3,2,1,0:T(8,128)(2,1)} %get-tuple-element.19), channel_id=1, source_target_pairs={{0,2},{2,4},{4,6},{6,8},{8,10},{10,12},{12,14},{14,16},{16,18},{18... | collective-permute-start | bytes 786440 | tf_op jit(solution)/shard_map/rows/ppermute | solution.py:311
  114.5 0.1 stack.38.refs_0_
  114.6 0.0 collective-permute-done.3.refs_6_
  114.6 1.9 %collective-permute-start.4 = (bf16[2,2,256,128]{3,2,1,0:T(8,128)(2,1)S(1)}, bf16[2,2,256,128]{3,2,1,0:T(8,128)(2,1)}, u32[]{:S(2)}, u32[]{:S(2)}) collective-permute-start(bf16[2,2,256,128]{3,2,1,0:T(8,128)(2,1)S(1)} %collective-permute-done.3.refs_6_), channel_id=1, source_target_pairs={{0,2},{2,4},{4,6},{6,8},{8,10},{10,12},{12,14},{14,16},{16,18},{18... | collective-permute-start | bytes 786440 | tf_op jit(solution)/shard_map/rows/ppermute | solution.py:312
  116.5 0.0 collective-permute-done.5.refs_5_
  116.6 4.6 %collective-permute-start.6 = (bf16[2,2,256,128]{3,2,1,0:T(8,128)(2,1)S(1)}, bf16[2,2,256,128]{3,2,1,0:T(8,128)(2,1)}, u32[]{:S(2)}, u32[]{:S(2)}) collective-permute-start(bf16[2,2,256,128]{3,2,1,0:T(8,128)(2,1)S(1)} %collective-permute-done.5.refs_5_), channel_id=1, source_target_pairs={{0,30},{2,0},{4,2},{6,4},{8,6},{10,8},{12,10},{14,12},{16,14},{18,... | collective-permute-start | bytes 786440 | tf_op jit(solution)/shard_map/rows/ppermute | solution.py:312
  121.2 0.0 collective-permute-done.8.refs_4_
  121.2 0.8 collective-permute-done.9.refs_7_
  122.0 0.0 collective-permute-done.7.refs_10_.refs_11_
  122.0 1.6 copy-done.2
  123.6 5.8 %head_stats.3 = f32[8,256]{1,0:T(8,128)S(1)} custom-call(s32[7]{0:T(128)S(1)} %stack.38.refs_0_, f32[1,2048]{1,0:T(1,128)S(1)} %bitcast.51, f32[1,2048]{1,0:T(1,128)S(1)} %bitcast.53, f32[32,128]{1,0:T(8,128)S(1)} %fusion.3.refs_3_, bf16[2,2,256,128]{3,2,1,0:T(8,128)(2,1)S(1)} %collective-permute-done.8.refs_4_, ...), custom_call_target="tpu_custom_call" | custom-call | flops 2147483648 | bytes 8388608 | tf_op jit(solution)/shard_map/head/head_stats/pallas_call | solution.py:220
  129.4 0.1 reshape.45
  129.5 0.1 copy.25
  129.6 0.0 collective-permute-done.6.refs_6_
  129.6 0.0 copy-start.3
  129.6 1.6 copy-done.3
  131.2 5.9 %head_stats.2 = f32[8,256]{1,0:T(8,128)S(1)} custom-call(s32[7]{0:T(128)S(1)} %stack.38.refs_0_, f32[1,2048]{1,0:T(1,128)S(1)} %bitcast.52, f32[1,2048]{1,0:T(1,128)S(1)} %bitcast.54, f32[32,128]{1,0:T(8,128)S(1)} %fusion.3.refs_3_, bf16[4,2,256,128]{3,2,1,0:T(8,128)(2,1)S(1)} %bitcast.46, bf16[2,2,256,128]{3,2,1,0:T(8,128)(2,1)} %collective-permute-done.4.refs_5_, ...), custom_call_target="tpu_custom_call" | custom-call | flops 2147483648 | bytes 8388608 | tf_op jit(solution)/shard_map/head/head_stats/pallas_call | solution.py:220
  137.0 0.1 reshape.44
  137.1 0.1 copy.24
  137.2 0.1 copy.28
  137.3 28.9 %all_to_all.10 = f32[64,2,16]{2,1,0:T(2,128)S(1)} all-to-all(f32[64,2,16]{2,1,0:T(2,128)S(1)} %bitcast.55), channel_id=1, replica_groups=mesh['enc'=2,'blk'=8,'zq'=4,'zr'=4,'yhi'=2] {'enc','zq','zr','yhi'}, dimensions={0} | all-to-all | bytes 16384 | tf_op jit(solution)/shard_map/merge/all_to_all | solution.py:369
  166.2 0.1 reshape.47
  166.4 0.1 slice_reduce_fusion.1
  166.4 0.1 fusion.1
  166.5 0.6 reshape.48
  (22 shorter events, 0.2 us)
Async XLA Ops:
  2.1 64.1 %all-to-all-start = ((bf16[32,104,128]{2,1,0:T(8,128)(2,1)}), bf16[32,104,128]{2,1,0:T(8,128)(2,1)S(1)}, u32[]{:S(2)}, u32[]{:S(2)}) async-start(bf16[32,104,128]{2,1,0:T(8,128)(2,1)} %pack.1), calls=%async_computation | async-start | bytes 1703936 | tf_op jit(solution)/shard_map/spread/all_to_all | solution.py:278
  20.8 7.8 %collective-permute-start = (bf16[2048,512]{1,0:T(8,128)(2,1)}, bf16[2048,512]{1,0:T(8,128)(2,1)S(1)}, u32[]{:S(2)}, u32[]{:S(2)}) collective-permute-start(bf16[2048,512]{1,0:T(8,128)(2,1)} %refs_8_.1), channel_id=1, source_target_pairs={{0,256},{256,0},{1,257},{257,1},{2,258},{258,2},{3,259},{259,3},{4... | collective-permute-start | bytes 6291464 | tf_op jit(solution)/shard_map/weights/ppermute | solution.py:272
  23.7 75.2 %collective-permute-start.2 = (bf16[2048,512]{1,0:T(8,128)(2,1)}, bf16[2048,512]{1,0:T(8,128)(2,1)}, u32[]{:S(2)}, u32[]{:S(2)}) collective-permute-start(bf16[2048,512]{1,0:T(8,128)(2,1)} %refs_8_.1), channel_id=1, source_target_pairs={{0,1},{1,0},{2,3},{3,2},{4,5},{5,4},{6,7},{7,6},{8,9},{9,8},{10,11... | collective-permute-start | bytes 6291464 | tf_op jit(solution)/shard_map/weights/ppermute | solution.py:271
  28.6 38.1 %copy-start.1 = (bf16[2048,512]{1,0:T(8,128)(2,1)}, bf16[2048,512]{1,0:T(8,128)(2,1)S(1)}, u32[]{:S(2)}) copy-start(bf16[2048,512]{1,0:T(8,128)(2,1)S(1)} %collective-permute-done.refs_8_.refs_9_) | copy-start | bytes 6291460
  66.7 55.3 %copy-start = (bf16[2048,512]{1,0:T(8,128)(2,1)S(1)}, bf16[2048,512]{1,0:T(8,128)(2,1)}, u32[]{:S(2)}) copy-start(bf16[2048,512]{1,0:T(8,128)(2,1)} %refs_8_.1) | copy-start | bytes 6291460
  66.7 55.3 %copy-start.4 = (f32[2048]{0:T(1024)S(1)}, f32[2048]{0:T(1024)}, u32[]{:S(2)}) copy-start(f32[2048]{0:T(1024)} %param.17) | copy-start | bytes 24580
  66.8 55.2 %copy-start.5 = (f32[2048]{0:T(1024)S(1)}, f32[2048]{0:T(1024)}, u32[]{:S(2)}) copy-start(f32[2048]{0:T(1024)} %param.18) | copy-start | bytes 24580
  69.4 4.8 %collective-permute-start.1 = (bf16[256,128]{1,0:T(8,128)(2,1)S(1)}, bf16[256,128]{1,0:T(8,128)(2,1)S(1)}, u32[]{:S(2)}, u32[]{:S(2)}) collective-permute-start(bf16[256,128]{1,0:T(8,128)(2,1)S(1)} %get-tuple-element.22), channel_id=1, source_target_pairs={{0,256},{256,0},{1,257},{257,1},{2,258},{258,2},{3,259},{259,3},{4... | collective-permute-start | bytes 196616 | tf_op jit(solution)/shard_map/halves/ppermute | solution.py:302
  98.8 23.2 %collective-permute-start.7 = (bf16[2048,512]{1,0:T(8,128)(2,1)}, bf16[2048,512]{1,0:T(8,128)(2,1)}, u32[]{:S(2)}, u32[]{:S(2)}) collective-permute-start(bf16[2048,512]{1,0:T(8,128)(2,1)} %collective-permute-done.2.refs_9_.refs_10_), channel_id=1, source_target_pairs={{0,256},{256,0},{1,257},{257,1},{2,258},{258,2},{3,259},{259,3},{4... | collective-permute-start | bytes 6291464 | tf_op jit(solution)/shard_map/weights/ppermute | solution.py:314
  102.7 11.9 %collective-permute-start.3 = (bf16[2,2,256,128]{3,2,1,0:T(8,128)(2,1)}, bf16[2,2,256,128]{3,2,1,0:T(8,128)(2,1)S(1)}, u32[]{:S(2)}, u32[]{:S(2)}) collective-permute-start(bf16[2,2,256,128]{3,2,1,0:T(8,128)(2,1)} %get-tuple-element.20), channel_id=1, source_target_pairs={{0,2},{2,4},{4,6},{6,8},{8,10},{10,12},{12,14},{14,16},{16,18},{18... | collective-permute-start | bytes 786440 | tf_op jit(solution)/shard_map/rows/ppermute | solution.py:310
  104.6 11.9 %collective-permute-start.5 = (bf16[2,2,256,128]{3,2,1,0:T(8,128)(2,1)}, bf16[2,2,256,128]{3,2,1,0:T(8,128)(2,1)S(1)}, u32[]{:S(2)}, u32[]{:S(2)}) collective-permute-start(bf16[2,2,256,128]{3,2,1,0:T(8,128)(2,1)} %get-tuple-element.19), channel_id=1, source_target_pairs={{0,30},{2,0},{4,2},{6,4},{8,6},{10,8},{12,10},{14,12},{16,14},{18,... | collective-permute-start | bytes 786440 | tf_op jit(solution)/shard_map/rows/ppermute | solution.py:310
  109.2 11.9 %collective-permute-start.8 = (bf16[2,2,256,128]{3,2,1,0:T(8,128)(2,1)}, bf16[2,2,256,128]{3,2,1,0:T(8,128)(2,1)S(1)}, u32[]{:S(2)}, u32[]{:S(2)}) collective-permute-start(bf16[2,2,256,128]{3,2,1,0:T(8,128)(2,1)} %get-tuple-element.20), channel_id=1, source_target_pairs={{0,30},{2,0},{4,2},{6,4},{8,6},{10,8},{12,10},{14,12},{16,14},{18,... | collective-permute-start | bytes 786440 | tf_op jit(solution)/shard_map/rows/ppermute | solution.py:311
  111.6 10.4 %collective-permute-start.9 = (bf16[2,2,256,128]{3,2,1,0:T(8,128)(2,1)}, bf16[2,2,256,128]{3,2,1,0:T(8,128)(2,1)}, u32[]{:S(2)}, u32[]{:S(2)}) collective-permute-start(bf16[2,2,256,128]{3,2,1,0:T(8,128)(2,1)} %get-tuple-element.19), channel_id=1, source_target_pairs={{0,2},{2,4},{4,6},{6,8},{8,10},{10,12},{12,14},{14,16},{16,18},{18... | collective-permute-start | bytes 786440 | tf_op jit(solution)/shard_map/rows/ppermute | solution.py:311
  114.6 14.9 %collective-permute-start.4 = (bf16[2,2,256,128]{3,2,1,0:T(8,128)(2,1)S(1)}, bf16[2,2,256,128]{3,2,1,0:T(8,128)(2,1)}, u32[]{:S(2)}, u32[]{:S(2)}) collective-permute-start(bf16[2,2,256,128]{3,2,1,0:T(8,128)(2,1)S(1)} %collective-permute-done.3.refs_6_), channel_id=1, source_target_pairs={{0,2},{2,4},{4,6},{6,8},{8,10},{10,12},{12,14},{14,16},{16,18},{18... | collective-permute-start | bytes 786440 | tf_op jit(solution)/shard_map/rows/ppermute | solution.py:312
  116.6 13.0 %collective-permute-start.6 = (bf16[2,2,256,128]{3,2,1,0:T(8,128)(2,1)S(1)}, bf16[2,2,256,128]{3,2,1,0:T(8,128)(2,1)}, u32[]{:S(2)}, u32[]{:S(2)}) collective-permute-start(bf16[2,2,256,128]{3,2,1,0:T(8,128)(2,1)S(1)} %collective-permute-done.5.refs_5_), channel_id=1, source_target_pairs={{0,30},{2,0},{4,2},{6,4},{8,6},{10,8},{12,10},{14,12},{16,14},{18,... | collective-permute-start | bytes 786440 | tf_op jit(solution)/shard_map/rows/ppermute | solution.py:312
  122.0 1.6 copy-start.2
  129.6 1.6 copy-start.3

commit v6 on v5

--- a/solution.py
+++ b/solution.py
@@ -232,7 +232,7 @@
             pltpu.VMEM((128, 128), F32),
             pltpu.SemaphoreType.DMA((len(slabs),)),
         ],
-        compiler_params=pltpu.CompilerParams(vmem_limit_bytes=32 * MIB),
+        compiler_params=pltpu.CompilerParams(vmem_limit_bytes=50 * MIB),
         cost_estimate=pl.CostEstimate(
             flops=2 * rows * D * len(slabs) * width,
             bytes_accessed=2 * D * len(slabs) * width,

time: 168 us -> 166 us (0.988)
  local copies, waits for them, and re-layouts: 5.8 us -> 2.63 us
    unnamed x12 -> x8, local copies, waits for them, and re-layouts: 3.2 us -> 0.02 us
where the time goes in v6:
time: 166 us; the launch traced here: 165 us
  blocking collectives  53.6 us (32%)
  starting transfers between devices  51.6 us (31%)
  waiting for transfers between devices  39.3 us (24%)
  Pallas kernels  17.4 us (10%)
  local copies, waits for them, and re-layouts  2.63 us (2%)
    all_to_all x1, waiting for transfers between devices, per_device(): got = lax.all_to_all(message, VOC, 0, 0, tiled=True)  37.6 us
    all_to_all x1, blocking collectives, per_device(): lax.all_to_all(stats.reshape(enc_count * voc_count, 2, -1), ('enc',) + VO...  28.9 us
    all_gather x1, blocking collectives, per_device(): fours = lax.all_gather(shard, 'zq', axis=0)  24.7 us
    all_to_all x1, starting transfers between devices, per_device(): got = lax.all_to_all(message, VOC, 0, 0, tiled=True)  18.7 us
    pallas_call x2, Pallas kernels, head_stats(): pl.pallas_call(kernel, in_specs=[pl.BlockSpec(memory_space=pltpu.SMEM)] +...  12.8 us
    ppermute x1, starting transfers between devices, per_device(): weight_y = lax.ppermute(head_weight, 'yhi', SWAP)  4.93 us
    ppermute x1, starting transfers between devices, per_device(): lax.ppermute(above_high, Z, down)  4.57 us
    ppermute x1, starting transfers between devices, per_device(): lax.ppermute(high, Z, down)  4.57 us
  transfers between devices with their start and end apart: 11, of which 3 were waited for; matrix products, arithmetic and copies ran while one was open for 1% of the time, Pallas kernels for 5%

profile of v6, /device:TPU:1, one launch (start us, length us, event | category | flops | bytes accessed | tf_op | source)
XLA Modules:
  0.0 165.1 jit_solution(2291872985050271768)
XLA Ops:
  0.0 2.1 %pack.1 = bf16[32,104,128]{2,1,0:T(8,128)(2,1)} custom-call(bf16[64,1024]{1,0:T(8,128)(2,1)} %refs_0_.1, bf16[64,1024]{1,0:T(8,128)(2,1)} %refs_1_.1, bf16[32,1024]{1,0:T(8,128)(2,1)} %refs_2_.1, bf16[32,1024]{1,0:T(8,128)(2,1)} %refs_3_.1, s32[1,64]{1,0:T(1,128)} %bitcast.57, s32[1,32]{1,0:T(1,128)} %bitcast.58, s32[1,64]{1,0:T(1,128)} %bitcast.59), custom_call_target="tpu_custom_call" | custom-call | tf_op jit(solution)/shard_map/pack/pack/pallas_call | solution.py:75
  2.1 18.7 %all-to-all-start = ((bf16[32,104,128]{2,1,0:T(8,128)(2,1)}), bf16[32,104,128]{2,1,0:T(8,128)(2,1)S(1)}, u32[]{:S(2)}, u32[]{:S(2)}) async-start(bf16[32,104,128]{2,1,0:T(8,128)(2,1)} %pack.1), calls=%async_computation | async-start | bytes 1703936 | tf_op jit(solution)/shard_map/spread/all_to_all | solution.py:278
  20.8 2.9 %collective-permute-start = (bf16[2048,512]{1,0:T(8,128)(2,1)}, bf16[2048,512]{1,0:T(8,128)(2,1)S(1)}, u32[]{:S(2)}, u32[]{:S(2)}) collective-permute-start(bf16[2048,512]{1,0:T(8,128)(2,1)} %refs_8_.1), channel_id=1, source_target_pairs={{0,256},{256,0},{1,257},{257,1},{2,258},{258,2},{3,259},{259,3},{4... | collective-permute-start | bytes 6291464 | tf_op jit(solution)/shard_map/weights/ppermute | solution.py:272
  23.6 4.9 %collective-permute-start.2 = (bf16[2048,512]{1,0:T(8,128)(2,1)}, bf16[2048,512]{1,0:T(8,128)(2,1)}, u32[]{:S(2)}, u32[]{:S(2)}) collective-permute-start(bf16[2048,512]{1,0:T(8,128)(2,1)} %refs_8_.1), channel_id=1, source_target_pairs={{0,1},{1,0},{2,3},{3,2},{4,5},{5,4},{6,7},{7,6},{8,9},{9,8},{10,11... | collective-permute-start | bytes 6291464 | tf_op jit(solution)/shard_map/weights/ppermute | solution.py:271
  28.6 0.0 collective-permute-done.refs_8_.refs_9_
  28.6 0.0 copy-start.3
  28.6 37.6 %all-to-all-done = bf16[32,104,128]{2,1,0:T(8,128)(2,1)S(1)} async-done(((bf16[32,104,128]{2,1,0:T(8,128)(2,1)}), bf16[32,104,128]{2,1,0:T(8,128)(2,1)S(1)}, u32[]{:S(2)}, u32[]{:S(2)}) %all-to-all-start) | async-done | bytes 852000 | tf_op jit(solution)/shard_map/spread/all_to_all | solution.py:278
  66.2 0.1 copy.22
  66.4 0.1 constant_dynamic-slice_fusion.1
  66.4 0.2 reshape.50.refs_4_
  66.6 0.1 squeeze.15.refs_5_
  66.7 0.0 copy-start
  66.7 0.0 copy-start.1
  66.7 0.0 copy-start.2
  66.8 2.5 %attend.1 = bf16[2,256,128]{2,1,0:T(8,128)(2,1)S(1)} custom-call(bf16[512,128]{1,0:T(8,128)(2,1)S(1)} %bitcast.50, bf16[512,128]{1,0:T(8,128)(2,1)S(1)} %bitcast.49, bf16[1024,128]{1,0:T(8,128)(2,1)S(1)} %bitcast.48, bf16[1024,128]{1,0:T(8,128)(2,1)S(1)} %bitcast.47, s32[512,1]{1,0:T(8,128)S(1)} %reshape.50.refs_4_, s32[1,1024]{1,0:T(1,128)S(1)} %squeeze.15.refs_5_), custom_call_target="tpu_custom_call" | custom-call | tf_op jit(solution)/shard_map/attention/attend/pallas_call | solution.py:113
  69.4 3.9 %collective-permute-start.1 = (bf16[256,128]{1,0:T(8,128)(2,1)S(1)}, bf16[256,128]{1,0:T(8,128)(2,1)S(1)}, u32[]{:S(2)}, u32[]{:S(2)}) collective-permute-start(bf16[256,128]{1,0:T(8,128)(2,1)S(1)} %get-tuple-element.22), channel_id=1, source_target_pairs={{0,256},{256,0},{1,257},{257,1},{2,258},{258,2},{3,259},{259,3},{4... | collective-permute-start | bytes 196616 | tf_op jit(solution)/shard_map/halves/ppermute | solution.py:302
  73.2 0.9 collective-permute-done.1
  74.1 24.7 %all-gather = bf16[8,256,128]{2,1,0:T(8,128)(2,1)S(1)} all-gather(bf16[2,256,128]{2,1,0:T(8,128)(2,1)S(1)} %pad_maximum_fusion), channel_id=2, replica_groups=mesh['enc'=2,'blk'=8,'zq'=4,'zr'=4,'yhi'=2] {'zq'}, dimensions={0}, use_global_device_ids=true | all-gather | bytes 655360 | tf_op jit(solution)/shard_map/rows/all_gather | solution.py:306
  98.8 0.0 collective-permute-done.2.refs_9_.refs_10_
  98.8 3.0 %collective-permute-start.7 = (bf16[2048,512]{1,0:T(8,128)(2,1)}, bf16[2048,512]{1,0:T(8,128)(2,1)}, u32[]{:S(2)}, u32[]{:S(2)}) collective-permute-start(bf16[2048,512]{1,0:T(8,128)(2,1)} %collective-permute-done.2.refs_9_.refs_10_), channel_id=1, source_target_pairs={{0,256},{256,0},{1,257},{257,1},{2,258},{258,2},{3,259},{259,3},{4... | collective-permute-start | bytes 6291464 | tf_op jit(solution)/shard_map/weights/ppermute | solution.py:314
  101.9 0.8 fusion.8
  102.7 1.9 %collective-permute-start.3 = (bf16[2,2,256,128]{3,2,1,0:T(8,128)(2,1)}, bf16[2,2,256,128]{3,2,1,0:T(8,128)(2,1)S(1)}, u32[]{:S(2)}, u32[]{:S(2)}) collective-permute-start(bf16[2,2,256,128]{3,2,1,0:T(8,128)(2,1)} %get-tuple-element.20), channel_id=1, source_target_pairs={{0,2},{2,4},{4,6},{6,8},{8,10},{10,12},{12,14},{14,16},{16,18},{18... | collective-permute-start | bytes 786440 | tf_op jit(solution)/shard_map/rows/ppermute | solution.py:310
  104.6 4.6 %collective-permute-start.5 = (bf16[2,2,256,128]{3,2,1,0:T(8,128)(2,1)}, bf16[2,2,256,128]{3,2,1,0:T(8,128)(2,1)S(1)}, u32[]{:S(2)}, u32[]{:S(2)}) collective-permute-start(bf16[2,2,256,128]{3,2,1,0:T(8,128)(2,1)} %get-tuple-element.19), channel_id=1, source_target_pairs={{0,30},{2,0},{4,2},{6,4},{8,6},{10,8},{12,10},{14,12},{16,14},{18,... | collective-permute-start | bytes 786440 | tf_op jit(solution)/shard_map/rows/ppermute | solution.py:310
  109.2 2.4 %collective-permute-start.8 = (bf16[2,2,256,128]{3,2,1,0:T(8,128)(2,1)}, bf16[2,2,256,128]{3,2,1,0:T(8,128)(2,1)S(1)}, u32[]{:S(2)}, u32[]{:S(2)}) collective-permute-start(bf16[2,2,256,128]{3,2,1,0:T(8,128)(2,1)} %get-tuple-element.20), channel_id=1, source_target_pairs={{0,30},{2,0},{4,2},{6,4},{8,6},{10,8},{12,10},{14,12},{16,14},{18,... | collective-permute-start | bytes 786440 | tf_op jit(solution)/shard_map/rows/ppermute | solution.py:311
  111.6 2.9 %collective-permute-start.9 = (bf16[2,2,256,128]{3,2,1,0:T(8,128)(2,1)}, bf16[2,2,256,128]{3,2,1,0:T(8,128)(2,1)}, u32[]{:S(2)}, u32[]{:S(2)}) collective-permute-start(bf16[2,2,256,128]{3,2,1,0:T(8,128)(2,1)} %get-tuple-element.19), channel_id=1, source_target_pairs={{0,2},{2,4},{4,6},{6,8},{8,10},{10,12},{12,14},{14,16},{16,18},{18... | collective-permute-start | bytes 786440 | tf_op jit(solution)/shard_map/rows/ppermute | solution.py:311
  114.5 0.1 stack.38.refs_0_
  114.6 0.0 collective-permute-done.3.refs_6_
  114.6 1.9 %collective-permute-start.4 = (bf16[2,2,256,128]{3,2,1,0:T(8,128)(2,1)S(1)}, bf16[2,2,256,128]{3,2,1,0:T(8,128)(2,1)}, u32[]{:S(2)}, u32[]{:S(2)}) collective-permute-start(bf16[2,2,256,128]{3,2,1,0:T(8,128)(2,1)S(1)} %collective-permute-done.3.refs_6_), channel_id=1, source_target_pairs={{0,2},{2,4},{4,6},{6,8},{8,10},{10,12},{12,14},{14,16},{16,18},{18... | collective-permute-start | bytes 786440 | tf_op jit(solution)/shard_map/rows/ppermute | solution.py:312
  116.5 0.0 collective-permute-done.5.refs_5_
  116.6 4.6 %collective-permute-start.6 = (bf16[2,2,256,128]{3,2,1,0:T(8,128)(2,1)S(1)}, bf16[2,2,256,128]{3,2,1,0:T(8,128)(2,1)}, u32[]{:S(2)}, u32[]{:S(2)}) collective-permute-start(bf16[2,2,256,128]{3,2,1,0:T(8,128)(2,1)S(1)} %collective-permute-done.5.refs_5_), channel_id=1, source_target_pairs={{0,30},{2,0},{4,2},{6,4},{8,6},{10,8},{12,10},{14,12},{16,14},{18,... | collective-permute-start | bytes 786440 | tf_op jit(solution)/shard_map/rows/ppermute | solution.py:312
  121.2 0.0 collective-permute-done.8.refs_4_
  121.2 0.8 collective-permute-done.9.refs_7_
  122.0 0.0 collective-permute-done.7.refs_10_.refs_11_
  122.0 0.0 copy-done.1
  122.0 6.4 %head_stats.3 = f32[8,256]{1,0:T(8,128)S(1)} custom-call(s32[7]{0:T(128)S(1)} %stack.38.refs_0_, f32[1,2048]{1,0:T(1,128)S(1)} %bitcast.51, f32[1,2048]{1,0:T(1,128)S(1)} %bitcast.53, f32[32,128]{1,0:T(8,128)S(1)} %fusion.3.refs_3_, bf16[2,2,256,128]{3,2,1,0:T(8,128)(2,1)S(1)} %collective-permute-done.8.refs_4_, ...), custom_call_target="tpu_custom_call" | custom-call | flops 2147483648 | bytes 8388608 | tf_op jit(solution)/shard_map/head/head_stats/pallas_call | solution.py:220
  128.4 0.1 reshape.45
  128.5 0.1 copy.25
  128.5 0.0 collective-permute-done.4.refs_5_
  128.5 0.0 collective-permute-done.6.refs_6_
  128.5 6.4 %head_stats.2 = f32[8,256]{1,0:T(8,128)S(1)} custom-call(s32[7]{0:T(128)S(1)} %stack.38.refs_0_, f32[1,2048]{1,0:T(1,128)S(1)} %bitcast.52, f32[1,2048]{1,0:T(1,128)S(1)} %bitcast.54, f32[32,128]{1,0:T(8,128)S(1)} %fusion.3.refs_3_, bf16[4,2,256,128]{3,2,1,0:T(8,128)(2,1)S(1)} %bitcast.46, bf16[2,2,256,128]{3,2,1,0:T(8,128)(2,1)} %collective-permute-done.4.refs_5_, ...), custom_call_target="tpu_custom_call" | custom-call | flops 2147483648 | bytes 8388608 | tf_op jit(solution)/shard_map/head/head_stats/pallas_call | solution.py:220
  135.0 0.1 reshape.44
  135.1 0.1 copy.24
  135.2 0.1 copy.28
  135.3 28.9 %all_to_all.10 = f32[64,2,16]{2,1,0:T(2,128)S(1)} all-to-all(f32[64,2,16]{2,1,0:T(2,128)S(1)} %bitcast.55), channel_id=1, replica_groups=mesh['enc'=2,'blk'=8,'zq'=4,'zr'=4,'yhi'=2] {'enc','zq','zr','yhi'}, dimensions={0} | all-to-all | bytes 16384 | tf_op jit(solution)/shard_map/merge/all_to_all | solution.py:369
  164.2 0.1 reshape.47
  164.3 0.1 slice_reduce_fusion.1
  164.4 0.1 fusion.1
  164.5 0.6 reshape.48
  (18 shorter events, 0.2 us)
Async XLA Ops:
  2.1 64.1 %all-to-all-start = ((bf16[32,104,128]{2,1,0:T(8,128)(2,1)}), bf16[32,104,128]{2,1,0:T(8,128)(2,1)S(1)}, u32[]{:S(2)}, u32[]{:S(2)}) async-start(bf16[32,104,128]{2,1,0:T(8,128)(2,1)} %pack.1), calls=%async_computation | async-start | bytes 1703936 | tf_op jit(solution)/shard_map/spread/all_to_all | solution.py:278
  20.8 7.8 %collective-permute-start = (bf16[2048,512]{1,0:T(8,128)(2,1)}, bf16[2048,512]{1,0:T(8,128)(2,1)S(1)}, u32[]{:S(2)}, u32[]{:S(2)}) collective-permute-start(bf16[2048,512]{1,0:T(8,128)(2,1)} %refs_8_.1), channel_id=1, source_target_pairs={{0,256},{256,0},{1,257},{257,1},{2,258},{258,2},{3,259},{259,3},{4... | collective-permute-start | bytes 6291464 | tf_op jit(solution)/shard_map/weights/ppermute | solution.py:272
  23.6 75.2 %collective-permute-start.2 = (bf16[2048,512]{1,0:T(8,128)(2,1)}, bf16[2048,512]{1,0:T(8,128)(2,1)}, u32[]{:S(2)}, u32[]{:S(2)}) collective-permute-start(bf16[2048,512]{1,0:T(8,128)(2,1)} %refs_8_.1), channel_id=1, source_target_pairs={{0,1},{1,0},{2,3},{3,2},{4,5},{5,4},{6,7},{7,6},{8,9},{9,8},{10,11... | collective-permute-start | bytes 6291464 | tf_op jit(solution)/shard_map/weights/ppermute | solution.py:271
  28.6 38.1 %copy-start.3 = (bf16[2048,512]{1,0:T(8,128)(2,1)}, bf16[2048,512]{1,0:T(8,128)(2,1)S(1)}, u32[]{:S(2)}) copy-start(bf16[2048,512]{1,0:T(8,128)(2,1)S(1)} %collective-permute-done.refs_8_.refs_9_) | copy-start | bytes 6291460
  66.7 55.3 %copy-start = (bf16[2048,512]{1,0:T(8,128)(2,1)S(1)}, bf16[2048,512]{1,0:T(8,128)(2,1)}, u32[]{:S(2)}) copy-start(bf16[2048,512]{1,0:T(8,128)(2,1)} %refs_8_.1) | copy-start | bytes 6291460
  66.7 55.3 %copy-start.1 = (f32[2048]{0:T(1024)S(1)}, f32[2048]{0:T(1024)}, u32[]{:S(2)}) copy-start(f32[2048]{0:T(1024)} %param.17) | copy-start | bytes 24580
  66.7 55.3 %copy-start.2 = (f32[2048]{0:T(1024)S(1)}, f32[2048]{0:T(1024)}, u32[]{:S(2)}) copy-start(f32[2048]{0:T(1024)} %param.18) | copy-start | bytes 24580
  69.4 4.8 %collective-permute-start.1 = (bf16[256,128]{1,0:T(8,128)(2,1)S(1)}, bf16[256,128]{1,0:T(8,128)(2,1)S(1)}, u32[]{:S(2)}, u32[]{:S(2)}) collective-permute-start(bf16[256,128]{1,0:T(8,128)(2,1)S(1)} %get-tuple-element.22), channel_id=1, source_target_pairs={{0,256},{256,0},{1,257},{257,1},{2,258},{258,2},{3,259},{259,3},{4... | collective-permute-start | bytes 196616 | tf_op jit(solution)/shard_map/halves/ppermute | solution.py:302
  98.8 23.2 %collective-permute-start.7 = (bf16[2048,512]{1,0:T(8,128)(2,1)}, bf16[2048,512]{1,0:T(8,128)(2,1)}, u32[]{:S(2)}, u32[]{:S(2)}) collective-permute-start(bf16[2048,512]{1,0:T(8,128)(2,1)} %collective-permute-done.2.refs_9_.refs_10_), channel_id=1, source_target_pairs={{0,256},{256,0},{1,257},{257,1},{2,258},{258,2},{3,259},{259,3},{4... | collective-permute-start | bytes 6291464 | tf_op jit(solution)/shard_map/weights/ppermute | solution.py:314
  102.7 11.9 %collective-permute-start.3 = (bf16[2,2,256,128]{3,2,1,0:T(8,128)(2,1)}, bf16[2,2,256,128]{3,2,1,0:T(8,128)(2,1)S(1)}, u32[]{:S(2)}, u32[]{:S(2)}) collective-permute-start(bf16[2,2,256,128]{3,2,1,0:T(8,128)(2,1)} %get-tuple-element.20), channel_id=1, source_target_pairs={{0,2},{2,4},{4,6},{6,8},{8,10},{10,12},{12,14},{14,16},{16,18},{18... | collective-permute-start | bytes 786440 | tf_op jit(solution)/shard_map/rows/ppermute | solution.py:310
  104.6 11.9 %collective-permute-start.5 = (bf16[2,2,256,128]{3,2,1,0:T(8,128)(2,1)}, bf16[2,2,256,128]{3,2,1,0:T(8,128)(2,1)S(1)}, u32[]{:S(2)}, u32[]{:S(2)}) collective-permute-start(bf16[2,2,256,128]{3,2,1,0:T(8,128)(2,1)} %get-tuple-element.19), channel_id=1, source_target_pairs={{0,30},{2,0},{4,2},{6,4},{8,6},{10,8},{12,10},{14,12},{16,14},{18,... | collective-permute-start | bytes 786440 | tf_op jit(solution)/shard_map/rows/ppermute | solution.py:310
  109.2 11.9 %collective-permute-start.8 = (bf16[2,2,256,128]{3,2,1,0:T(8,128)(2,1)}, bf16[2,2,256,128]{3,2,1,0:T(8,128)(2,1)S(1)}, u32[]{:S(2)}, u32[]{:S(2)}) collective-permute-start(bf16[2,2,256,128]{3,2,1,0:T(8,128)(2,1)} %get-tuple-element.20), channel_id=1, source_target_pairs={{0,30},{2,0},{4,2},{6,4},{8,6},{10,8},{12,10},{14,12},{16,14},{18,... | collective-permute-start | bytes 786440 | tf_op jit(solution)/shard_map/rows/ppermute | solution.py:311
  111.6 10.4 %collective-permute-start.9 = (bf16[2,2,256,128]{3,2,1,0:T(8,128)(2,1)}, bf16[2,2,256,128]{3,2,1,0:T(8,128)(2,1)}, u32[]{:S(2)}, u32[]{:S(2)}) collective-permute-start(bf16[2,2,256,128]{3,2,1,0:T(8,128)(2,1)} %get-tuple-element.19), channel_id=1, source_target_pairs={{0,2},{2,4},{4,6},{6,8},{8,10},{10,12},{12,14},{14,16},{16,18},{18... | collective-permute-start | bytes 786440 | tf_op jit(solution)/shard_map/rows/ppermute | solution.py:311
  114.6 13.9 %collective-permute-start.4 = (bf16[2,2,256,128]{3,2,1,0:T(8,128)(2,1)S(1)}, bf16[2,2,256,128]{3,2,1,0:T(8,128)(2,1)}, u32[]{:S(2)}, u32[]{:S(2)}) collective-permute-start(bf16[2,2,256,128]{3,2,1,0:T(8,128)(2,1)S(1)} %collective-permute-done.3.refs_6_), channel_id=1, source_target_pairs={{0,2},{2,4},{4,6},{6,8},{8,10},{10,12},{12,14},{14,16},{16,18},{18... | collective-permute-start | bytes 786440 | tf_op jit(solution)/shard_map/rows/ppermute | solution.py:312
  116.6 12.0 %collective-permute-start.6 = (bf16[2,2,256,128]{3,2,1,0:T(8,128)(2,1)S(1)}, bf16[2,2,256,128]{3,2,1,0:T(8,128)(2,1)}, u32[]{:S(2)}, u32[]{:S(2)}) collective-permute-start(bf16[2,2,256,128]{3,2,1,0:T(8,128)(2,1)S(1)} %collective-permute-done.5.refs_5_), channel_id=1, source_target_pairs={{0,30},{2,0},{4,2},{6,4},{8,6},{10,8},{12,10},{14,12},{16,14},{18,... | collective-permute-start | bytes 786440 | tf_op jit(solution)/shard_map/rows/ppermute | solution.py:312
